TPU v7x, 128 devices: a whole 4x4x4 slice. The times are simulated.
128 devices in a mesh: dp: 32 (over z, y_lo, x), cls: 4 (over y_hi, core).
Axes of the slice: x: 4, y: 4 (y_hi: 2, y_lo: 2; y = y_hi * 2 + y_lo), z: 4, core: 2. Of those that a mesh axis runs over, the one named last changes fastest.
Arguments:
- particles: bfloat16 [256, 2, 288, 128], P('dp'), may hold values from -20 to 20
- references: bfloat16 [288, 2, 200, 128], P('dp', None, 'cls'), may hold values from -9 to 9
- ctf_table: float32 [16, 128], replicated, may hold values from -0.1 to 0.1
- rot_offset: int32 [200], P('cls'), may hold values from 0 to 7
- prior_shift: int32 [256, 2], P('dp'), may hold values from -8 to 8
- defocus_group: int32 [256], P('dp'), may hold values from 0 to 15
Outputs:
- log_evidence: float32 [256], P('dp')
- class_posterior: float32 [256, 200], P('dp', 'cls')
- class_sums: float32 [288, 2, 200, 128], P('dp', None, 'cls')
All inputs are finite; a program needn't handle non-finite values.
Results may differ from a plain program's by a relative error of at most 0.0056.
Values may be sent and summed in bfloat16 or wider, within the bound.
A program may use at most 384 MiB of HBM per device.

v0:
```python
import math

import jax
import jax.numpy as jnp
from jax import lax
from jax.sharding import PartitionSpec as P

ROTS = 36
ANG_STEP = 8
SHIFT_SIDE = 5


two_pi = 2.0 * math.pi


def fourier_rows(angles):
    index_grid = jnp.arange(angles, dtype=jnp.int32)
    phase_index = index_grid[:, None] * index_grid[None, :] % angles
    radians = phase_index.astype(jnp.float32) * (two_pi / angles)
    cosine = jnp.cos(radians)
    sine_part = jnp.sin(radians)
    table_full = jnp.stack(
        [jnp.stack([cosine, sine_part], 1), jnp.stack([-sine_part, cosine], 1)], 1
    )
    return table_full.reshape(2 * angles, 2 * angles).astype(jnp.bfloat16)


def rotation_tables(freq_rows, offsets, angles):
    rotation_steps = jnp.arange(ROTS, dtype=jnp.int32) * ANG_STEP
    angle_grid = rotation_steps[None, :] + offsets[:, None]
    phase_index = freq_rows[:, None, None] * angle_grid[None, :, :] % angles
    radians = phase_index.astype(jnp.float32) * (two_pi / angles)
    return (jnp.cos(radians), jnp.sin(radians))


def local(particles, references, ctf_table, rot_offset, prior_shift, defocus_group):
    top_score_value = lax.Precision.HIGHEST
    particle_count = particles.shape[0]
    angles = particles.shape[2]
    cycles = particles.shape[3]
    classes_here = references.shape[2]
    group_count = ctf_table.shape[0]
    shifts = SHIFT_SIDE * SHIFT_SIDE
    queries = particle_count * shifts
    shift_index = jnp.arange(shifts, dtype=jnp.int32)
    along_x = shift_index // SHIFT_SIDE - SHIFT_SIDE // 2
    along_y = shift_index % SHIFT_SIDE - SHIFT_SIDE // 2
    theta_grid = jnp.arange(angles, dtype=jnp.int32).astype(jnp.float32) * (two_pi / angles)
    radius = (jnp.arange(cycles, dtype=jnp.int32) + 1).astype(jnp.float32) / (2.0 * cycles)
    table_wide = fourier_rows(angles)
    onehot = (defocus_group[:, None] == jnp.arange(group_count, dtype=jnp.int32)[None, :]).astype(
        jnp.float32
    )
    ctf_rows = jnp.dot(onehot, ctf_table, precision=top_score_value)

    def transform(inputs):
        image, offset, ctf_row = inputs
        shift_x = (offset[0] + along_x).astype(jnp.float32)
        shift_y = (offset[1] + along_y).astype(jnp.float32)
        argument = (
            two_pi
            * radius[None, None, :]
            * (
                shift_x[None, :, None] * jnp.cos(theta_grid)[:, None, None]
                + shift_y[None, :, None] * jnp.sin(theta_grid)[:, None, None]
            )
        )
        cosine = jnp.cos(argument)
        sine_part = jnp.sin(argument)
        real_part = image[0].astype(jnp.float32)[:, None, :]
        imag_part = image[1].astype(jnp.float32)[:, None, :]
        shifted = jnp.stack(
            [real_part * cosine + imag_part * sine_part, imag_part * cosine - real_part * sine_part]
        ).astype(jnp.bfloat16)
        spectrum = jnp.dot(
            table_wide,
            shifted.reshape(2 * angles, shifts * cycles),
            preferred_element_type=jnp.float32,
        )
        spectrum = spectrum.reshape(angles, 2, shifts, cycles) * ctf_row[None, None, None, :]
        return spectrum.astype(jnp.bfloat16)

    per_particle = lax.map(transform, (particles, prior_shift, ctf_rows))
    weighted = jnp.transpose(per_particle, (1, 2, 0, 3, 4)).reshape(angles, 2, queries, cycles)
    shard_piece = lax.all_gather(references, "dp", axis=0, tiled=True)
    rows_here = shard_piece.shape[0]
    query_block = weighted.reshape(rows_here, 2 * queries, cycles)
    class_block = shard_piece.reshape(rows_here, 2 * classes_here, cycles)
    product = lax.dot_general(
        query_block, class_block, (((2,), (2,)), ((0,), (0,))), preferred_element_type=jnp.float32
    )
    product = product.reshape(rows_here, 2, queries, 2, classes_here)
    real_correlation = product[:, 0, :, 0] + product[:, 1, :, 1]
    imag_correlation = product[:, 1, :, 0] - product[:, 0, :, 1]
    freq_rows = jnp.arange(rows_here, dtype=jnp.int32)
    cos_table, sin_table = rotation_tables(freq_rows, rot_offset, angles)
    stacked_table = jnp.transpose(jnp.concatenate([cos_table, -sin_table], 0), (1, 0, 2))
    stacked_corr = jnp.transpose(
        jnp.concatenate([real_correlation, imag_correlation], 0), (2, 1, 0)
    )
    cross_sums = lax.dot_general(
        stacked_corr, stacked_table, (((2,), (1,)), ((0,), (0,))), precision=top_score_value
    )
    piece_values = shard_piece.astype(jnp.float32)
    cycle_power = jnp.sum(piece_values * piece_values, axis=(0, 1))
    power_sums = jnp.dot(cycle_power, (ctf_table * ctf_table).T, precision=top_score_value)
    cross_sums, power_sums = (cross_sums, power_sums)
    class_power = jnp.dot(onehot, power_sums.T, precision=top_score_value)
    cross_ordered = jnp.transpose(cross_sums, (1, 0, 2))
    scores = (
        cross_ordered.reshape(particle_count, shifts, classes_here, ROTS) / angles
        - 0.5 * class_power[:, None, :, None] / angles
    )
    local_peak = jnp.max(scores, axis=(1, 2, 3))
    peak_score = lax.pmax(local_peak, "cls")
    total_mass = lax.psum(
        jnp.sum(jnp.exp(scores - peak_score[:, None, None, None]), axis=(1, 2, 3)), "cls"
    )
    log_evidence = peak_score + jnp.log(total_mass)
    weights = jnp.exp(scores - log_evidence[:, None, None, None])
    class_posterior = jnp.sum(weights, axis=(1, 3))
    class_weights = jnp.transpose(weights.reshape(queries, classes_here, ROTS), (1, 0, 2))
    own_rows = angles // lax.axis_size("dp")
    freq_rows = jnp.arange(angles, dtype=jnp.int32)
    cos_table, sin_table = rotation_tables(freq_rows, rot_offset, angles)
    stacked_table = jnp.transpose(jnp.concatenate([cos_table, sin_table], 0), (1, 2, 0))
    returned = lax.dot_general(
        class_weights, stacked_table, (((2,), (1,)), ((0,), (0,))), precision=top_score_value
    ).astype(jnp.bfloat16)
    real_returned = jnp.transpose(returned[:, :, :angles], (2, 1, 0))
    imag_returned = jnp.transpose(returned[:, :, angles:], (2, 1, 0))
    mixing = jnp.stack(
        [
            jnp.stack([real_returned, -imag_returned], 1),
            jnp.stack([imag_returned, real_returned], 1),
        ],
        1,
    )
    query_block = weighted
    summed = lax.psum(
        lax.dot_general(
            mixing,
            query_block,
            (((2, 3), (1, 2)), ((0,), (0,))),
            preferred_element_type=jnp.float32,
        ),
        "dp",
    )
    class_sums = lax.dynamic_slice_in_dim(summed, lax.axis_index("dp") * own_rows, own_rows, 0)
    return (log_evidence, class_posterior, class_sums)


def solution(mesh):
    placed = (
        P("dp", None, None, None),
        P("dp", None, "cls", None),
        P(),
        P("cls"),
        P("dp", None),
        P("dp"),
    )
    return jax.shard_map(
        local,
        mesh=mesh,
        in_specs=placed,
        out_specs=(P("dp"), P("dp", "cls"), P("dp", None, "cls", None)),
        check_vma=False,
    )
```

profile of v0, /device:TPU:0, one launch (start us, length us, event | category | flops | bytes accessed | tf_op | source)
XLA Modules:
  0.0 1197.7 jit_solution(17716305374547799971)
XLA Ops:
  8.0 1.9 negate_convert_fusion
  9.9 1.8 fusion.72
  13.5 15.9 %fusion.55 = (f32[288,50,36]{0,2,1:T(8,128)}, f32[288,50,36]{0,2,1:T(8,128)}, f32[288,50,36]{0,2,1:T(8,128)}) fusion(s32[50,36]{1,0:T(8,128)S(1)} %broadcast_add_fusion), kind=kLoop, calls=%fused_computation.83 | loop fusion | flops 5184000 | bytes 6228000 | tf_op jit(solution)/shard_map/sin | solution.py:33
  29.5 381.1 %while.13 = (s32[]{:T(128)}, bf16[8,288,2,25,128]{4,1,3,0,2:T(8,128)(2,1)}, bf16[8,2,288,128]{3,2,1,0:T(8,128)(2,1)}, s32[8,2]{0,1:T(2,128)S(1)}, bf16[576,576]{...) while((s32[]{:T(128)}, ...), condition=%wide.region_1.2_spmd.clone, body=%wide.region_0.1_spmd.clone.sunk | while | flops 2137287680 | bytes 56820304 | solution.py:83
  30.6 1.3 fusion.99
  33.3 18.5 %fusion.100 = (bf16[1,288,25,128]{3,2,1,0:T(8,128)(2,1)S(1)}, bf16[1,288,25,128]{3,2,1,0:T(8,128)(2,1)S(1)}) fusion(f32[288,128]{1,0:T(8,128)S(1)} %get-tuple-element.241, f32[288,25]{1,0:T(8,128)S(1)} %copy.127, f32[128]{0:T(128)S(1)} %convert_multiply_fusion.3, f32[288,128]{1,0:T(8,128)S(1)} %get-tuple-element.246), kind=kLoop, calls=%fused_computation.14.clone.1 | loop fusion | flops 8294400 | bytes 4010624 | tf_op jit(solution)/shard_map/convert.2
  52.5 6.7 convolution_bitcast_fusion.2
  59.1 9.1 reshape.331
  68.3 5.0 multiply_convert_fusion.2
  73.3 4.3 copy_dynamic-update-slice_fusion.2
  78.3 1.3 fusion.99
  80.9 18.5 %fusion.100 = (bf16[1,288,25,128]{3,2,1,0:T(8,128)(2,1)S(1)}, bf16[1,288,25,128]{3,2,1,0:T(8,128)(2,1)S(1)}) fusion(f32[288,128]{1,0:T(8,128)S(1)} %get-tuple-element.241, f32[288,25]{1,0:T(8,128)S(1)} %copy.127, f32[128]{0:T(128)S(1)} %convert_multiply_fusion.3, f32[288,128]{1,0:T(8,128)S(1)} %get-tuple-element.246), kind=kLoop, calls=%fused_computation.14.clone.1 | loop fusion | flops 8294400 | bytes 4010624 | tf_op jit(solution)/shard_map/convert.2
  100.1 6.7 convolution_bitcast_fusion.2
  106.8 9.2 reshape.331
  115.9 5.0 multiply_convert_fusion.2
  121.0 4.2 copy_dynamic-update-slice_fusion.2
  128.5 18.5 %fusion.100 = (bf16[1,288,25,128]{3,2,1,0:T(8,128)(2,1)S(1)}, bf16[1,288,25,128]{3,2,1,0:T(8,128)(2,1)S(1)}) fusion(f32[288,128]{1,0:T(8,128)S(1)} %get-tuple-element.241, f32[288,25]{1,0:T(8,128)S(1)} %copy.127, f32[128]{0:T(128)S(1)} %convert_multiply_fusion.3, f32[288,128]{1,0:T(8,128)S(1)} %get-tuple-element.246), kind=kLoop, calls=%fused_computation.14.clone.1 | loop fusion | flops 8294400 | bytes 4010624 | tf_op jit(solution)/shard_map/convert.2
  147.6 6.7 convolution_bitcast_fusion.2
  154.3 9.1 reshape.331
  163.4 5.1 multiply_convert_fusion.2
  168.6 4.4 copy_dynamic-update-slice_fusion.2
  173.5 1.3 fusion.99
  176.2 18.5 %fusion.100 = (bf16[1,288,25,128]{3,2,1,0:T(8,128)(2,1)S(1)}, bf16[1,288,25,128]{3,2,1,0:T(8,128)(2,1)S(1)}) fusion(f32[288,128]{1,0:T(8,128)S(1)} %get-tuple-element.241, f32[288,25]{1,0:T(8,128)S(1)} %copy.127, f32[128]{0:T(128)S(1)} %convert_multiply_fusion.3, f32[288,128]{1,0:T(8,128)S(1)} %get-tuple-element.246), kind=kLoop, calls=%fused_computation.14.clone.1 | loop fusion | flops 8294400 | bytes 4010624 | tf_op jit(solution)/shard_map/convert.2
  195.3 6.7 convolution_bitcast_fusion.2
  202.0 9.1 reshape.331
  211.1 5.0 multiply_convert_fusion.2
  216.1 4.3 copy_dynamic-update-slice_fusion.2
  223.7 18.5 %fusion.100 = (bf16[1,288,25,128]{3,2,1,0:T(8,128)(2,1)S(1)}, bf16[1,288,25,128]{3,2,1,0:T(8,128)(2,1)S(1)}) fusion(f32[288,128]{1,0:T(8,128)S(1)} %get-tuple-element.241, f32[288,25]{1,0:T(8,128)S(1)} %copy.127, f32[128]{0:T(128)S(1)} %convert_multiply_fusion.3, f32[288,128]{1,0:T(8,128)S(1)} %get-tuple-element.246), kind=kLoop, calls=%fused_computation.14.clone.1 | loop fusion | flops 8294400 | bytes 4010624 | tf_op jit(solution)/shard_map/convert.2
  242.9 6.7 convolution_bitcast_fusion.2
  249.6 9.1 reshape.331
  258.7 5.0 multiply_convert_fusion.2
  263.7 4.3 copy_dynamic-update-slice_fusion.2
  271.3 18.5 %fusion.100 = (bf16[1,288,25,128]{3,2,1,0:T(8,128)(2,1)S(1)}, bf16[1,288,25,128]{3,2,1,0:T(8,128)(2,1)S(1)}) fusion(f32[288,128]{1,0:T(8,128)S(1)} %get-tuple-element.241, f32[288,25]{1,0:T(8,128)S(1)} %copy.127, f32[128]{0:T(128)S(1)} %convert_multiply_fusion.3, f32[288,128]{1,0:T(8,128)S(1)} %get-tuple-element.246), kind=kLoop, calls=%fused_computation.14.clone.1 | loop fusion | flops 8294400 | bytes 4010624 | tf_op jit(solution)/shard_map/convert.2
  290.4 6.7 convolution_bitcast_fusion.2
  297.1 9.1 reshape.331
  306.2 5.0 multiply_convert_fusion.2
  311.2 4.3 copy_dynamic-update-slice_fusion.2
  318.8 18.5 %fusion.100 = (bf16[1,288,25,128]{3,2,1,0:T(8,128)(2,1)S(1)}, bf16[1,288,25,128]{3,2,1,0:T(8,128)(2,1)S(1)}) fusion(f32[288,128]{1,0:T(8,128)S(1)} %get-tuple-element.241, f32[288,25]{1,0:T(8,128)S(1)} %copy.127, f32[128]{0:T(128)S(1)} %convert_multiply_fusion.3, f32[288,128]{1,0:T(8,128)S(1)} %get-tuple-element.246), kind=kLoop, calls=%fused_computation.14.clone.1 | loop fusion | flops 8294400 | bytes 4010624 | tf_op jit(solution)/shard_map/convert.2
  338.0 6.7 convolution_bitcast_fusion.2
  344.6 9.1 reshape.331
  353.7 5.0 multiply_convert_fusion.2
  358.8 4.4 copy_dynamic-update-slice_fusion.2
  366.4 18.5 %fusion.100 = (bf16[1,288,25,128]{3,2,1,0:T(8,128)(2,1)S(1)}, bf16[1,288,25,128]{3,2,1,0:T(8,128)(2,1)S(1)}) fusion(f32[288,128]{1,0:T(8,128)S(1)} %get-tuple-element.241, f32[288,25]{1,0:T(8,128)S(1)} %copy.127, f32[128]{0:T(128)S(1)} %convert_multiply_fusion.3, f32[288,128]{1,0:T(8,128)S(1)} %get-tuple-element.246), kind=kLoop, calls=%fused_computation.14.clone.1 | loop fusion | flops 8294400 | bytes 4010624 | tf_op jit(solution)/shard_map/convert.2
  385.6 6.7 convolution_bitcast_fusion.2
  392.2 9.1 reshape.331
  401.3 5.0 multiply_convert_fusion.2
  406.4 4.2 copy_dynamic-update-slice_fusion.2
  410.6 7.2 copy.84
  417.8 37.8 %fusion.31 = f32[288,400,100]{2,1,0:T(8,128)} fusion(bf16[288,400,128]{2,0,1:T(8,128)(2,1)} %bitcast.123, bf16[288,100,128]{2,0,1:T(8,128)(2,1)} %bitcast.125), kind=kOutput, calls=%fused_computation.47 | convolution fusion | flops 2949120000 | bytes 82944000 | tf_op jit(solution)/shard_map/dot_general | solution.py:89
  455.6 68.2 %copy.87 = f32[288,400,100]{0,1,2:T(8,128)} copy(f32[288,400,100]{2,1,0:T(8,128)} %fusion.31) | data formatting | bytes 92160000 | tf_op jit(solution)/shard_map/dot_general | solution.py:89
  523.9 30.8 %fusion.39 = (f32[288,200,50]{0,1,2:T(8,128)}, f32[288,200,50]{0,1,2:T(8,128)}) fusion(f32[288,2,200,2,50]{0,2,1,4,3:T(8,128)} %bitcast.121), kind=kLoop, calls=%fused_computation.59 | loop fusion | flops 5760000 | bytes 69120000 | tf_op jit(solution)/shard_map/add | solution.py:93
  554.7 9.4 multiply_reduce_fusion
  564.6 36.0 %fusion.62 = (f32[200]{0:T(256)S(1)}, f32[50,200,36]{1,2,0:T(8,128)S(1)}) fusion(f32[200,50]{0,1:T(8,128)S(1)} %copy.92, f32[288,50,36]{0,2,1:T(8,128)} %get-tuple-element.191, f32[288,50,36]{0,2,1:T(8,128)} %get-tuple-element.190, f32[288,200,50]{0,1,2:T(8,128)} %get-tuple-element.182, f32[288,200,50]{0,1,2:T(8,128)} %get-tuple-element.181), kind=kOutput, calls=%fused_computation.93 | convolution fusion | flops 2496196608 | bytes 28668000 | tf_op jit(solution)/shard_map/dot_general | solution.py:101
  600.8 9.8 pmax.7
  611.5 7.5 psum.14
  619.2 26.7 %convolution_convert_fusion = bf16[50,200,576]{2,1,0:T(8,128)(2,1)S(1)} fusion(f32[288,50,36]{0,2,1:T(8,128)} %get-tuple-element.191, f32[288,50,36]{0,2,1:T(8,128)} %get-tuple-element.189, f32[50,200,36]{1,2,0:T(8,128)S(1)} %get-tuple-element.193, f32[200]{0:T(256)S(1)} %sub.97, f32[50,200]{1,0:T(8,128)S(1)} %copy.94), kind=kOutput, calls=%fused_computation.64 | convolution fusion | flops 2496196864 | bytes 17148000 | tf_op jit(solution)/shard_map/dot_general | solution.py:127
  646.0 4.6 copy-done
  650.6 7.3 slice_bitcast_fusion.5
  657.8 9.0 fusion.43
  666.8 25.1 %maximum_bitcast_fusion.2 = (bf16[288,1,2,200,50]{0,3,4,2,1:T(8,128)(2,1)}, bf16[288,1,2,200,50]{0,3,4,2,1:T(8,128)(2,1)}) fusion(bf16[288,1,200,50]{0,2,3,1:T(8,128)(2,1)} %fusion.43, bf16[288,1,200,50]{0,2,3,1:T(8,128)(2,1)} %get-tuple-element.184, bf16[288,1,200,50]{0,2,3,1:T(8,128)(2,1)} %get-tuple-element.183), kind=kLoop, calls=%fused_computation.61 | loop fusion | flops 11520000 | bytes 40320000 | tf_op jit(solution)/shard_map/stack | solution.py:132
  691.9 21.4 %pad_maximum_fusion.1 = bf16[288,2,2,200,50]{0,3,4,2,1:T(8,128)(2,1)} fusion(bf16[288,1,2,200,50]{0,3,4,2,1:T(8,128)(2,1)} %get-tuple-element.186, bf16[288,1,2,200,50]{0,3,4,2,1:T(8,128)(2,1)} %get-tuple-element.185), kind=kLoop, calls=%fused_computation.44 | loop fusion | flops 11520000 | bytes 46080000 | tf_op jit(solution)/shard_map/stack | solution.py:132
  713.3 50.3 %copy.95 = bf16[288,2,2,200,50]{3,4,2,1,0:T(8,128)(2,1)} copy(bf16[288,2,2,200,50]{0,3,4,2,1:T(8,128)(2,1)} %pad_maximum_fusion.1) | data formatting | bytes 46080000 | tf_op jit(solution)/shard_map/stack | solution.py:132
  763.6 32.2 %fusion.40 = f32[288,2,50,128]{3,2,1,0:T(8,128)} fusion(bf16[288,2,2,200,50]{3,4,2,1,0:T(8,128)(2,1)} %copy.95, bf16[288,2,200,128,1]{3,0,2,1,4:T(8,128)(2,1)} %bitcast.124), kind=kOutput, calls=%fused_computation.65 | convolution fusion | flops 2949120000 | bytes 67276800 | tf_op jit(solution)/shard_map/dot_general | solution.py:141
  797.1 391.1 %all-reduce.2.cloned.1.call-done = f32[288,2,50,128]{3,2,1,0:T(8,128)} async-done(((f32[288,2,50,128]{3,2,1,0:T(8,128)}), f32[288,2,50,128]{3,2,1,0:T(8,128)}) %all-reduce.2.cloned.1.call-update) | async-done | bytes 14745616 | tf_op jit(solution)/shard_map/psum | solution.py:140
  (135 shorter events, 34.8 us)
Async XLA Ops:
  7.2 6.2 copy-start.5
  7.2 403.4 %all-gather.2.cloned.1.call-start = ((), (), s32[]{:S(2)}) async-start(), calls=%async_computation | async-start | bytes 7603200 | tf_op jit(solution)/shard_map/all_gather | solution.py:85
  7.9 1180.3 %all-reduce.2.cloned.1.call-start = ((), (), s32[]{:S(2)}) async-start(), calls=%async_computation.1 | async-start | bytes 33030144 | tf_op jit(solution)/shard_map/psum | solution.py:140
  12.7 16.6 %copy-start.2 = (f32[16,128]{1,0:T(8,128)S(1)}, f32[16,128]{1,0:T(8,128)}, u32[]{:S(2)}) copy-start(f32[16,128]{1,0:T(8,128)} %param.10) | copy-start | bytes 24580
  12.7 16.6 %copy-start.6 = (s32[8]{0:T(128)S(1)}, s32[8]{0:T(128)}, u32[]{:S(2)}) copy-start(s32[8]{0:T(128)} %param.13) | copy-start | bytes 100
  12.7 16.8 %copy-start.1 = (s32[8,2]{0,1:T(2,128)S(1)}, s32[8,2]{0,1:T(2,128)}, u32[]{:S(2)}) copy-start(s32[8,2]{0,1:T(2,128)} %param.12) | copy-start | bytes 196
  554.7 9.4 copy-start.3
  554.7 9.6 copy-start.7
  619.0 27.0 %copy-start.4 = (f32[8]{0:T(128)}, f32[8]{0:T(128)S(1)}, u32[]{:S(2)}) copy-start(f32[8]{0:T(128)S(1)} %log_add_fusion) | copy-start | bytes 100
  646.0 4.6 copy-start
Sparse Core Ops, SparseCore 0:
  9.7 168.0 all-gather.1
  795.9 392.2 all-reduce.1
where the time goes:
time: 1210 us; the launch traced here: 1200 us
  waiting for transfers between devices  392 us (32%)
  other arithmetic  331 us (27%)
  local copies, waits for them, and re-layouts  255 us (21%)
  matrix products  187 us (15%)
  blocking collectives  17.3 us (1%)
  between operations  14.8 us (1%)
    psum x1, waiting for transfers between devices, local(): lax.psum(lax.dot_general(mixing, query_block, (((2, 3), (1, 2)), ((0,), (...  391 us
    another operation x10, other arithmetic  152 us
    reshape x8, local copies, waits for them, and re-layouts, transform(): spectrum.reshape(angles, 2, shifts, cycles) * ctf_row[None, None, None, :]  72.9 us
    dot_general x1, local copies, waits for them, and re-layouts, local(): lax.dot_general(query_block, class_block, (((2,), (2,)), ((0,), (0,))), p...  68.2 us
    dot_general x8, matrix products, transform(): jnp.dot(table_wide, shifted.reshape(2 * angles, shifts * cycles), preferr...  53.4 us
    another operation x1, local copies, waits for them, and re-layouts, local(): jnp.stack([jnp.stack([real_returned, -imag_returned], 1), jnp.stack([imag...  50.3 us
    another operation x2, other arithmetic, local(): jnp.stack([jnp.stack([real_returned, -imag_returned], 1), jnp.stack([imag...  46.5 us
    convert_element_type x8, other arithmetic, transform(): return spectrum.astype(jnp.bfloat16)  40.3 us
  transfers between devices with their start and end apart: 2, of which 1 were waited for; matrix products, arithmetic and copies ran while one was open for 34% of the time, Pallas kernels for 0%

commit v1 on v0

v1 whole, which is shorter than its diff:
```python
import functools
import heapq
import math

import jax
import jax.numpy as jnp
import numpy as np
from jax import lax
from jax.experimental import pallas as pl
from jax.experimental.pallas import tpu as pltpu
from jax.sharding import PartitionSpec as P

ROTS = 36
SIDE = 5
SHIFTS = SIDE * SIDE
ANGLES = 288
CYCLES = 128
HALF = ANGLES // 2
REACH = 10
FOLD = ROTS // 2 + 1
IPAD = 80
QROWS = 208
CPAD = 64
F32 = jnp.float32
BF16 = jnp.bfloat16
MESH = pl.DeviceIdType.MESH


def phase_tables():
    order = np.concatenate([np.arange(0, ANGLES, 2), np.arange(1, ANGLES, 2)])
    theta = 2.0 * np.pi * order / ANGLES
    radius = (np.arange(CYCLES) + 1) / (2.0 * CYCLES)
    count = np.arange(REACH + 1)
    out = []
    for wave in (np.cos(theta), np.sin(theta)):
        arg = 2.0 * np.pi * count[:, None, None] * wave[None, :, None] * radius[None, None, :]
        out.append(np.stack([np.cos(arg), np.sin(arg)], 1).astype(np.float32))
    return out


def dft_tables():
    row = np.arange(IPAD)
    out = []
    for start in (0, 1):
        t = np.arange(start, ANGLES, 2)
        ang = 2.0 * np.pi * ((row[:, None] * t[None, :]) % ANGLES) / ANGLES
        out.append(np.concatenate([np.cos(ang), np.sin(ang)], 0).astype(np.float32))
    return out


def rotation_coefs():
    k = np.arange(FOLD)
    ang = 2.0 * np.pi * ((k[:, None] * k[None, :]) % ROTS) / ROTS
    cos, sin = np.cos(ang), np.sin(ang)
    lanes = np.arange(128) < CPAD
    fwd = np.where(lanes, cos[:, :, None], -sin[:, :, None]) / ANGLES
    bwd = np.where(lanes, cos[:, :, None], sin[:, :, None])
    return fwd.astype(np.float32), bwd.astype(np.float32)


def transform_kernel(shift, part, ctf, tx, ty, te, to, out, z1, xs, fr, fi):
    u = pl.program_id(0)

    def row(j, carry):
        s = jnp.minimum(2 * u + j // 8, SHIFTS - 1)
        p = j % 8
        a = s // SIDE
        b = s % SIDE

        @pl.when((b == 0))
        def _():
            sx = shift[p, 0] + a - SIDE // 2
            n = jnp.abs(sx)
            sg = jnp.where(sx < 0, -1.0, 1.0).astype(F32)
            for c in range(0, ANGLES, 48):
                rows = pl.ds(c, 48)
                re = part[p, 0, rows, :].astype(F32)
                im = part[p, 1, rows, :].astype(F32)
                co = tx[n, 0, rows, :]
                si = tx[n, 1, rows, :] * sg
                z1[p, 0, rows, :] = re * co + im * si
                z1[p, 1, rows, :] = im * co - re * si

        sy = shift[p, 1] + b - SIDE // 2
        n = jnp.abs(sy)
        sg = jnp.where(sy < 0, -1.0, 1.0).astype(F32)
        for c in range(0, ANGLES, 48):
            rows = pl.ds(c, 48)
            re = z1[p, 0, rows, :]
            im = z1[p, 1, rows, :]
            co = ty[n, 0, rows, :]
            si = ty[n, 1, rows, :] * sg
            xs[rows, 0:128] = (re * co + im * si).astype(BF16)
            xs[rows, 128:256] = (im * co - re * si).astype(BF16)
        even = jnp.dot(te[...], xs[0:HALF, :], preferred_element_type=F32)
        odd = jnp.dot(to[...], xs[HALF:, :], preferred_element_type=F32)
        gain = ctf[pl.ds(p, 1), :]
        for c in range(0, IPAD, 16):
            ce = even[c : c + 16] * jnp.concatenate([gain, gain], 1)
            se = even[IPAD + c : IPAD + c + 16] * jnp.concatenate([gain, gain], 1)
            co = odd[c : c + 16] * jnp.concatenate([gain, gain], 1)
            so = odd[IPAD + c : IPAD + c + 16] * jnp.concatenate([gain, gain], 1)
            u1 = ce[:, :128] + se[:, 128:]
            u2 = ce[:, :128] - se[:, 128:]
            v1 = co[:, :128] + so[:, 128:]
            v2 = co[:, :128] - so[:, 128:]
            w1 = ce[:, 128:] - se[:, :128]
            w2 = ce[:, 128:] + se[:, :128]
            y1 = co[:, 128:] - so[:, :128]
            y2 = co[:, 128:] + so[:, :128]
            for blk, (re, im) in enumerate(
                ((u1 + v1, w1 + y1), (u1 - v1, w1 - y1), (u2 - v2, w2 - y2), (u2 + v2, w2 + y2))
            ):
                at = pl.ds((blk * IPAD + c) * 16 + j, 16, stride=16)
                fr[at, :] = re
                fi[at, :] = im
        return carry

    lax.fori_loop(0, 16, row, 0)

    def emit(i, blk, m):
        at = pl.ds(pl.multiple_of((blk * IPAD + i) * 16, 16), 16)
        out[m, :, 0:128] = fr[at, :].astype(BF16)
        out[m, :, 128:256] = fi[at, :].astype(BF16)

    def pack(i, carry):
        emit(i, 0, i)
        emit(i, 1, HALF + i)
        emit(i, 2, HALF - i)
        emit(i, 3, ANGLES - i)
        return carry

    emit(0, 0, 0)
    emit(0, 1, HALF)
    emit(HALF // 2, 0, HALF // 2)
    emit(HALF // 2, 1, HALF + HALF // 2)
    lax.fori_loop(1, HALF // 2, pack, 0, unroll=2)


def transform(shift, part, ctf):
    tx, ty = phase_tables()
    te, to = dft_tables()
    whole = pl.BlockSpec(memory_space=pltpu.VMEM)
    return pl.pallas_call(
        transform_kernel,
        grid=(QROWS // 16,),
        out_shape=jax.ShapeDtypeStruct((ANGLES, QROWS, 256), BF16),
        in_specs=[pl.BlockSpec(memory_space=pltpu.SMEM)] + [whole] * 6,
        out_specs=pl.BlockSpec((ANGLES, 16, 256), lambda u: (0, u, 0)),
        scratch_shapes=[
            pltpu.VMEM((8, 2, ANGLES, 128), F32),
            pltpu.VMEM((ANGLES, 256), BF16),
            pltpu.VMEM((4 * IPAD * 16, 128), F32),
            pltpu.VMEM((4 * IPAD * 16, 128), F32),
        ],
        compiler_params=pltpu.CompilerParams(vmem_limit_bytes=56 * 2**20),
        name="transform",
    )(shift, part, ctf, jnp.asarray(tx), jnp.asarray(ty), jnp.asarray(te, BF16), jnp.asarray(to, BF16))


def match_kernel(block, wt, refs, ctf, fwd, bwd, spec, peak, mass, post, acc, power):
    d = pl.program_id(0)

    @pl.when(d == 0)
    def _():
        acc[...] = jnp.zeros_like(acc)
        power[...] = jnp.zeros_like(power)

    for i in range(block):
        m = d * block + i
        r = m % ROTS
        up = r <= ROTS // 2
        g = jnp.where(up, r, ROTS - r)
        sg = jnp.where(up, 1.0, -1.0).astype(BF16)
        ar = refs[0, 0, i]
        ai = refs[0, 1, i]
        table = jnp.concatenate(
            [jnp.concatenate([ar, ai], 1), jnp.concatenate([-ai * sg, ar * sg], 1)], 0
        )
        acc[g] += lax.dot_general(
            wt[i], table, (((1,), (1,)), ((), ())), preferred_element_type=F32
        )
        fa = ar.astype(F32)
        fb = ai.astype(F32)
        power[...] += fa * fa + fb * fb

    @pl.when(d == pl.num_programs(0) - 1)
    def _():
        gain = ctf[...]
        half = lax.dot_general(
            gain * gain,
            power[...],
            (((1,), (1,)), ((), ())),
            precision=lax.Precision.HIGHEST,
            preferred_element_type=F32,
        ) * (0.5 / ANGLES)
        bias = jnp.concatenate([half, half], 1)
        lane = lax.broadcasted_iota(jnp.int32, (8, 128), 1)
        live = lane % CPAD < classes_of
        edge = lane < classes_of
        sign = jnp.where(lane < CPAD, 1.0, -1.0).astype(F32)
        low = -1e30

        def score(s, top):
            rows = pl.ds(pl.multiple_of(s * 8, 8), 8)
            parts = [acc[g, rows, :] for g in range(FOLD)]
            for k in range(FOLD):
                y = parts[0] * fwd[k, 0:1, :]
                for g in range(1, FOLD):
                    y = y + parts[g] * fwd[k, g : g + 1, :]
                y = y * sign + pltpu.roll(y, CPAD, 1) - bias
                y = jnp.where(edge if k in (0, FOLD - 1) else live, y, low)
                spec[k, rows, :] = y
                top = jnp.maximum(top, y)
            return top

        top = lax.fori_loop(0, SHIFTS, score, jnp.full((8, 128), low, F32))
        top = jnp.max(top, axis=1, keepdims=True)

        def weigh(s, total):
            rows = pl.ds(pl.multiple_of(s * 8, 8), 8)
            parts = []
            for k in range(FOLD):
                e = jnp.exp(spec[k, rows, :] - top)
                total = total + e
                parts.append(e * sign + pltpu.roll(e, CPAD, 1))
            for g in range(FOLD):
                y = parts[0] * bwd[g, 0:1, :]
                for k in range(1, FOLD):
                    y = y + parts[k] * bwd[g, k : k + 1, :]
                spec[g, rows, :] = y
            return total

        total = lax.fori_loop(0, SHIFTS, weigh, jnp.zeros((8, 128), F32))
        spec[:, SHIFTS * 8 :, :] = jnp.zeros((FOLD, QROWS - SHIFTS * 8, 128), F32)
        peak[...] = jnp.broadcast_to(top, (8, 128))
        mass[...] = jnp.broadcast_to(jnp.sum(total, axis=1, keepdims=True), (8, 128))
        post[...] = total + pltpu.roll(total, CPAD, 1)


classes_of = 50


def match(wt, refs, ctf):
    fwd, bwd = rotation_coefs()
    owners, _, block = refs.shape[:3]
    small = jax.ShapeDtypeStruct((8, 128), F32)
    whole = pl.BlockSpec(memory_space=pltpu.VMEM)
    return pl.pallas_call(
        functools.partial(match_kernel, block),
        grid=(owners,),
        out_shape=(jax.ShapeDtypeStruct((FOLD, QROWS, 128), F32), small, small, small),
        in_specs=[
            pl.BlockSpec((block, QROWS, 256), lambda d: (d, 0, 0)),
            pl.BlockSpec((1, 2, block, CPAD, 128), lambda d: (d, 0, 0, 0, 0)),
            whole,
            whole,
            whole,
        ],
        out_specs=(whole,) * 4,
        scratch_shapes=[pltpu.VMEM((FOLD, QROWS, 128), F32), pltpu.VMEM((CPAD, 128), F32)],
        compiler_params=pltpu.CompilerParams(vmem_limit_bytes=48 * 2**20),
        name="match",
    )(wt, refs, ctf, jnp.asarray(fwd), jnp.asarray(bwd))


def back_kernel(block, wt, spec, scale, out, tab):
    d = pl.program_id(0)

    @pl.when(d == 0)
    def _():
        for g in range(FOLD):
            rows = spec[g] * jnp.concatenate([scale[...]] * (QROWS // 8), 0)
            tab[g] = rows.T.astype(BF16)

    for i in range(block):
        m = d * block + i
        r = m % ROTS
        up = r <= ROTS // 2
        g = jnp.where(up, r, ROTS - r)
        sg = jnp.where(up, 1.0, -1.0).astype(F32)
        both = jnp.dot(tab[g], wt[i], preferred_element_type=F32)
        out[0, 0, i] = (both[:CPAD, :128] - sg * both[CPAD:, 128:]).astype(BF16)
        out[0, 1, i] = (both[:CPAD, 128:] + sg * both[CPAD:, :128]).astype(BF16)


def back(wt, spec, scale, owners):
    block = ANGLES // owners
    whole = pl.BlockSpec(memory_space=pltpu.VMEM)
    return pl.pallas_call(
        functools.partial(back_kernel, block),
        grid=(owners,),
        out_shape=jax.ShapeDtypeStruct((owners, 2, block, CPAD, 128), BF16),
        in_specs=[pl.BlockSpec((block, QROWS, 256), lambda d: (d, 0, 0)), whole, whole],
        out_specs=pl.BlockSpec((1, 2, block, CPAD, 128), lambda d: (d, 0, 0, 0, 0)),
        scratch_shapes=[pltpu.VMEM((FOLD, 128, QROWS), BF16)],
        compiler_params=pltpu.CompilerParams(vmem_limit_bytes=48 * 2**20),
        name="back",
    )(wt, spec, scale)


def twist_tables(freq, rot_offset):
    idx = (freq[:, None] * rot_offset[None, :]) % ANGLES
    rad = idx.astype(F32) * (2.0 * math.pi / ANGLES)
    return jnp.cos(rad)[:, :, None], jnp.sin(rad)[:, :, None]


def twist_refs(references, cos, sin):
    re = references[:, 0].astype(F32)
    im = references[:, 1].astype(F32)
    both = jnp.stack([re * cos + im * sin, im * cos - re * sin], 0)
    return jnp.pad(both, ((0, 0), (0, 0), (0, CPAD - both.shape[2]), (0, 0))).astype(BF16)


def untwist(sums, cos, sin, classes):
    re = sums[0, :, :classes].astype(F32)
    im = sums[1, :, :classes].astype(F32)
    return jnp.stack([re * cos - im * sin, re * sin + im * cos], 1)


def order_angles(particles):
    return jnp.concatenate([particles[:, :, 0::2], particles[:, :, 1::2]], 2)


def group_rows(defocus_group, ctf_table):
    hit = defocus_group[:, None] == jnp.arange(ctf_table.shape[0], dtype=jnp.int32)[None, :]
    return jnp.sum(jnp.where(hit[:, :, None], ctf_table[None], 0.0), 1)
SIZES = (4, 2, 4)
SUB = (5, 4)
LATE = 0.5


def place():
    dp = lax.axis_index("dp")
    return dp % 4, (dp // 4) % 2, dp // 8, lax.axis_index("cls")


def peer(me, rel):
    x, y, z, cls = me
    return ((((z + rel[2]) % 4) * 2 + (y + rel[1]) % 2) * 4 + (x + rel[0]) % 4, cls)


def slot(me, rel):
    return peer(me, rel)[0]


def toward(axis, sign):
    move = [0, 0, 0]
    move[axis] = sign
    return tuple(move)


def greet(me):
    barrier = pltpu.get_barrier_semaphore()
    moves = [toward(0, 1), toward(0, -1), toward(1, 1), toward(2, 1), toward(2, -1)]
    for move in moves:
        pl.semaphore_signal(barrier, inc=1, device_id=peer(me, move), device_id_type=MESH)
    pl.semaphore_wait(barrier, len(moves))


def axes_of(half):
    return (0, 1, 2) if half == 0 else (2, 1, 0)


def span(sub):
    return pl.ds(0, sum(SUB)) if sub is None else pl.ds(0 if sub == 0 else SUB[0], SUB[sub])


class Links:
    def __init__(self):
        self.free, self.heap, self.count = {}, [], 0

    def send(self, t, axis, sign, size, key):
        start = max(t, self.free.get((axis, sign), 0.0))
        self.free[(axis, sign)] = start + size
        self.push(start + size + LATE, key)

    def push(self, t, key):
        self.count += 1
        heapq.heappush(self.heap, (t, self.count, key))

    def pop(self):
        t, _, key = heapq.heappop(self.heap)
        return t, key


def gather_plan():
    links, plan, got = Links(), [], {}
    for half in (0, 1):
        links.push(0.0, (half, (0, 0, 0), None))
    while links.heap:
        t, key = links.pop()
        half, rel, sub = key
        order = axes_of(half)
        sends = []

        def go(axis, sign, sub):
            seen = list(rel)
            seen[axis] = (seen[axis] - sign) % SIZES[axis]
            there = (half, tuple(seen), sub)
            sends.append((half, rel, sub, axis, sign, there))
            links.send(t, axis, sign, 1.0 if sub is None else SUB[sub] / sum(SUB), there)

        got[half, rel] = got.get((half, rel), 0) + 1
        if sub is None or got[half, rel] == 2:
            last = max([i for i in range(3) if rel[order[i]]], default=-1)
            for i in range(2, last, -1):
                if order[i] == 1:
                    go(1, 1, None)
                else:
                    go(order[i], 1, None)
                    go(order[i], -1, None)
            if last >= 0 and order[last] != 1:
                if rel[order[last]] == 3:
                    go(order[last], 1, 0)
                elif rel[order[last]] == 1:
                    go(order[last], -1, 1)
        plan.append((t, None if rel == (0, 0, 0) else key, sends))
    return plan


def gather_keys():
    plan = gather_plan()
    recv = {step[1]: i for i, step in enumerate(s for s in plan if s[1] is not None)}
    return plan, recv


class Gather:
    def __init__(self, me, own, store, send_sem, recv_sem):
        self.me, self.own, self.store = me, own, store
        self.send_sem, self.recv_sem = send_sem, recv_sem
        self.plan, self.recv = gather_keys()
        self.sent = []

    def copy(self, index, half, rel, sub, axis, sign, there):
        where = span(sub)
        here = self.own.at[half, where] if rel == (0, 0, 0) else self.store.at[slot(self.me, rel), half, where]
        return pltpu.make_async_remote_copy(
            src_ref=here,
            dst_ref=self.store.at[slot(self.me, rel), half, where],
            send_sem=self.send_sem.at[index],
            recv_sem=self.recv_sem.at[self.recv[there]],
            device_id=peer(self.me, toward(axis, sign)),
            device_id_type=MESH,
        )

    def arrived(self, key):
        half, rel, sub = key
        here = self.store.at[slot(self.me, rel), half, span(sub)]
        pltpu.make_async_remote_copy(
            src_ref=here,
            dst_ref=here,
            send_sem=self.send_sem.at[0],
            recv_sem=self.recv_sem.at[self.recv[key]],
            device_id=peer(self.me, (1, 0, 0)),
            device_id_type=MESH,
        ).wait_recv()

    def step(self, item):
        _, key, sends = item
        if key is not None:
            self.arrived(key)
        for send in sends:
            copy = self.copy(len(self.sent), *send)
            copy.start()
            self.sent.append(copy)

    def finish(self):
        for copy in self.sent:
            copy.wait_send()


def gather_kernel(own, store, send_sem, recv_sem, own_sem):
    me = place()
    greet(me)
    keep = pltpu.make_async_copy(own, store.at[slot(me, (0, 0, 0))], own_sem)
    keep.start()
    work = Gather(me, own, store, send_sem, recv_sem)
    for item in work.plan:
        work.step(item)
    work.finish()
    keep.wait()


def gather(own):
    plan, recv = gather_keys()
    owners = SIZES[0] * SIZES[1] * SIZES[2]
    return pl.pallas_call(
        gather_kernel,
        out_shape=jax.ShapeDtypeStruct((owners,) + own.shape, own.dtype),
        in_specs=[pl.BlockSpec(memory_space=pltpu.VMEM)],
        out_specs=pl.BlockSpec(memory_space=pl.ANY),
        scratch_shapes=[
            pltpu.SemaphoreType.DMA((sum(len(s[2]) for s in plan),)),
            pltpu.SemaphoreType.DMA((len(recv),)),
            pltpu.SemaphoreType.DMA,
        ],
        compiler_params=pltpu.CompilerParams(
            collective_id=1, has_side_effects=True, vmem_limit_bytes=16 * 2**20
        ),
        name="gather",
    )(own)


COMBOS = [(ry, c) for ry in (1, 0) for c in (2, 1, 3, 0)]


def scatter_plan(ready=None):
    links, steps, got = Links(), [], set()
    done = set()

    def send(t, half, stage, combo, kind):
        order = axes_of(half)[::-1]
        axis = order[stage]
        sign = 1 if kind in ("a0", "l0", "l1", "y") else -1
        size = 1.0 if kind == "y" else SUB[int(kind[1])] / sum(SUB)
        msg = (half, stage, combo, kind)
        steps.append(("send", msg))
        links.send(t, axis, sign, size, msg)

    def first(t, half, stage, combo, k):
        if k == 2:
            send(t, half, stage, combo, "a0")
            send(t, half, stage, combo, "a1")
        elif k == 1:
            send(t, half, stage, combo, "l1")
        elif k == 3:
            send(t, half, stage, combo, "r0")

    def second(t, half, c):
        if (half, 0, (0, c), "s") in done and (half, 1, c, "y") in got:
            steps.append(("pair", (half, c)))
            done.add((half, 2, c))
            first(t, half, 2, None, c)
            if c == 1:
                relay(t, half, 2, None, "a0")
            if c == 3:
                relay(t, half, 2, None, "a1")
            if c == 0:
                total(t, half, 2, None)

    def have(half, stage, k):
        return stage == 0 or (half, 2, k) in done

    def relay(t, half, stage, combo, kind):
        k = 1 if kind == "a0" else 3
        if (half, stage, combo, kind) in got and have(half, stage, k):
            steps.append(("relay", (half, stage, combo, kind)))
            send(t, half, stage, combo, "l0" if kind == "a0" else "r1")

    def total(t, half, stage, combo):
        if all((half, stage, combo, kind) in got for kind in ("l0", "l1", "r0", "r1")) and have(
            half, stage, 0
        ):
            steps.append(("total", (half, stage, combo)))
            if stage == 0:
                done.add((half, 0, combo, "s"))
                if combo[0] == 1:
                    send(t, half, 1, combo[1], "y")
                else:
                    second(t, half, combo[1])

    for k in (2, 1, 3):
        for combo in COMBOS:
            for half in (0, 1):
                first(0.0, half, 0, combo, k)
    while links.heap:
        t, msg = links.pop()
        half, stage, combo, kind = msg
        steps.append(("wait", msg))
        got.add(msg)
        if kind == "y":
            second(t, half, combo)
        elif kind in ("a0", "a1"):
            relay(t, half, stage, combo, kind)
        else:
            total(t, half, stage, combo)
    return steps


def scatter_keys():
    steps = scatter_plan()
    return steps, {s[1]: i for i, s in enumerate(s for s in steps if s[0] == "send")}


class Scatter:
    def __init__(self, me, own, three, pair, out, send_sem, recv_sem):
        self.me, self.own, self.three, self.pair, self.out = me, own, three, pair, out
        self.send_sem, self.recv_sem = send_sem, recv_sem
        self.steps, self.index = scatter_keys()
        self.sent = []

    def group(self, stage, combo):
        return 8 if stage == 2 else COMBOS.index(combo)

    def mine(self, half, stage, combo, k):
        if stage == 2:
            return self.pair.at[half, k]
        order = axes_of(half)[::-1]
        rel = [0, 0, 0]
        rel[order[0]] = k
        rel[1] = combo[0]
        rel[order[2]] = combo[1]
        return self.own.at[slot(self.me, rel), half]

    def box(self, msg):
        half, stage, combo, kind = msg
        if kind == "y":
            return self.pair.at[half, combo]
        which = {"a": 0, "l": 1, "r": 2}[kind[0]]
        return self.three.at[half, self.group(stage, combo), which, span(int(kind[1]))]

    def source(self, msg):
        half, stage, combo, kind = msg
        if kind == "y":
            return self.three.at[half, self.group(0, (1, combo)), 1]
        where = span(int(kind[1]))
        if kind in ("a0", "a1"):
            return self.mine(half, stage, combo, 2).at[where]
        if kind == "l1":
            return self.mine(half, stage, combo, 1).at[where]
        if kind == "r0":
            return self.mine(half, stage, combo, 3).at[where]
        return self.three.at[half, self.group(stage, combo), 0, where]

    def copy(self, msg, src=None):
        half, stage, combo, kind = msg
        axis = axes_of(half)[::-1][stage]
        sign = 1 if kind in ("a0", "l0", "l1", "y") else -1
        i = self.index[msg]
        box = self.box(msg)
        return pltpu.make_async_remote_copy(
            src_ref=box if src is None else src,
            dst_ref=box,
            send_sem=self.send_sem.at[i],
            recv_sem=self.recv_sem.at[i],
            device_id=peer(self.me, toward(axis, sign)),
            device_id_type=MESH,
        )

    def add(self, dst, terms, count):
        def one(i, carry):
            value = terms[0][i].astype(F32)
            for term in terms[1:]:
                value = value + term[i].astype(F32)
            dst[i] = value.astype(dst.dtype)
            return carry

        lax.fori_loop(0, count, one, 0)

    def step(self, item):
        what, key = item
        if what == "send":
            copy = self.copy(key, self.source(key))
            copy.start()
            self.sent.append(copy)
        elif what == "wait":
            self.copy(key).wait_recv()
        elif what == "relay":
            half, stage, combo, kind = key
            box = self.box(key)
            mine = self.mine(half, stage, combo, 1 if kind == "a0" else 3).at[span(int(kind[1]))]
            self.add(box, (mine, box), SUB[int(kind[1])])
        elif what == "pair":
            half, c = key
            box = self.pair.at[half, c]
            self.add(box, (self.three.at[half, self.group(0, (0, c)), 1], box), sum(SUB))
        else:
            half, stage, combo = key
            left = self.three.at[half, self.group(stage, combo), 1]
            right = self.three.at[half, self.group(stage, combo), 2]
            mine = self.mine(half, stage, combo, 0)
            dst = self.out.at[half] if stage == 2 else left
            self.add(dst, (mine, left, right), sum(SUB))

    def finish(self):
        for copy in self.sent:
            copy.wait_send()


def scatter_kernel(own, out, three, pair, send_sem, recv_sem):
    me = place()
    greet(me)
    work = Scatter(me, own, three, pair, out, send_sem, recv_sem)
    for item in work.steps:
        work.step(item)
    work.finish()


def scatter(own):
    steps, index = scatter_keys()
    block = own.shape[2:]
    return pl.pallas_call(
        scatter_kernel,
        out_shape=jax.ShapeDtypeStruct((2,) + block, F32),
        in_specs=[pl.BlockSpec(memory_space=pltpu.VMEM)],
        out_specs=pl.BlockSpec(memory_space=pltpu.VMEM),
        scratch_shapes=[
            pltpu.VMEM((2, 9, 3) + block, BF16),
            pltpu.VMEM((2, 4) + block, BF16),
            pltpu.SemaphoreType.DMA((len(index),)),
            pltpu.SemaphoreType.DMA((len(index),)),
        ],
        compiler_params=pltpu.CompilerParams(
            collective_id=2, has_side_effects=True, vmem_limit_bytes=48 * 2**20
        ),
        name="scatter",
    )(own)


def local(particles, references, ctf_table, rot_offset, prior_shift, defocus_group):
    owners = lax.axis_size("dp")
    block, _, classes = references.shape[:3]
    freq = lax.axis_index("dp") * block + jnp.arange(block, dtype=jnp.int32)
    cos, sin = twist_tables(freq, rot_offset)
    refs = gather(twist_refs(references, cos, sin))
    ctf = group_rows(defocus_group, ctf_table)
    wt = transform(prior_shift, order_angles(particles), ctf)
    spec, peak, mass, post = match(wt, refs, ctf)
    top = lax.pmax(peak[:, 0], "cls")
    log_evidence = top + jnp.log(lax.psum(mass[:, 0] * jnp.exp(peak[:, 0] - top), "cls"))
    scale = jnp.exp(peak - log_evidence[:, None])
    sums = scatter(back(wt, spec, scale, owners))
    return (
        log_evidence,
        post[:, :classes] * scale[:, :classes],
        untwist(sums, cos, sin, classes),
    )


def solution(mesh):
    placed = (
        P("dp", None, None, None),
        P("dp", None, "cls", None),
        P(),
        P("cls"),
        P("dp", None),
        P("dp"),
    )
    return jax.shard_map(
        local,
        mesh=mesh,
        in_specs=placed,
        out_specs=(P("dp"), P("dp", "cls"), P("dp", None, "cls", None)),
        check_vma=False,
    )
```

time: 1210 us -> 317 us (0.26)
  waiting for transfers between devices: 392 us -> 0 us
  other arithmetic: 331 us -> 5.3 us
  Pallas kernels: 0 us -> 283 us
  local copies, waits for them, and re-layouts: 255 us -> 8.58 us
  matrix products: 187 us -> 0 us
  between operations: 14.8 us -> 0.75 us
    psum x1 -> x0, waiting for transfers between devices: 391 us -> none  [local(): lax.psum(lax.dot_general(mixing, query_block, (((2, 3), (1, 2)), ((0,), (...]
    pallas_call x0 -> x5, Pallas kernels: none -> 283 us  [the longest x1 101 us: transform(): pl.pallas_call(transform_kernel, grid=(QROWS // 16,), out_shape=jax.Shape...]
    another operation x23 -> x3, other arithmetic: 213 us -> 0.31 us
    dot_general x15 -> x0, matrix products: 187 us -> none  [the longest x8 53.4 us: transform(): jnp.dot(table_wide, shifted.reshape(2 * angles, shifts * cycles), preferr...]
    reshape x8 -> x0, local copies, waits for them, and re-layouts: 72.9 us -> none  [transform(): spectrum.reshape(angles, 2, shifts, cycles) * ctf_row[None, None, None, :]]
    dot_general x1 -> x0, local copies, waits for them, and re-layouts: 68.2 us -> none  [local(): lax.dot_general(query_block, class_block, (((2,), (2,)), ((0,), (0,))), p...]
    convert_element_type x24 -> x0, other arithmetic: 58.3 us -> none  [the longest x8 40.3 us: transform(): return spectrum.astype(jnp.bfloat16)]
    another operation x3 -> x0, local copies, waits for them, and re-layouts: 58.3 us -> none  [the longest x1 50.3 us: local(): jnp.stack([jnp.stack([real_returned, -imag_returned], 1), jnp.stack([imag...]
  transfers between devices with their start and end apart: 2 -> 0, of which waited for: 1 -> 0; matrix products, arithmetic and copies ran while one was open for 34% -> 0% of each run, Pallas kernels for 0% -> 0%
where the time goes in v1:
time: 317 us; the launch traced here: 315 us
  Pallas kernels  283 us (89%)
  blocking collectives  17 us (5%)
  local copies, waits for them, and re-layouts  8.58 us (3%)
  other arithmetic  5.3 us (2%)
    pallas_call x1, Pallas kernels, transform(): pl.pallas_call(transform_kernel, grid=(QROWS // 16,), out_shape=jax.Shape...  101 us
    pallas_call x1, Pallas kernels, scatter(): pl.pallas_call(scatter_kernel, out_shape=jax.ShapeDtypeStruct((2,) + bloc...  61.6 us
    pallas_call x1, Pallas kernels, gather(): pl.pallas_call(gather_kernel, out_shape=jax.ShapeDtypeStruct((owners,) +...  53.2 us
    pallas_call x1, Pallas kernels, match(): pl.pallas_call(functools.partial(match_kernel, block), grid=(owners,), ou...  39.1 us
    pallas_call x1, Pallas kernels, back(): pl.pallas_call(functools.partial(back_kernel, block), grid=(owners,), out...  28.9 us
    pmax x1, blocking collectives, local(): top = lax.pmax(peak[:, 0], 'cls')  8.9 us
    psum x1, blocking collectives, local(): lax.psum(mass[:, 0] * jnp.exp(peak[:, 0] - top), 'cls')  8.08 us

profile of v1, /device:TPU:0, one launch (start us, length us, event | category | flops | bytes accessed | tf_op | source)
XLA Modules:
  0.0 315.1 jit_solution(15854147796240030097)
XLA Ops:
  0.6 0.0 copy-start.4
  0.7 0.8 iota_compare_fusion.1
  1.5 1.4 select_reduce_fusion.ctf
  2.9 1.3 copy.23.shift
  4.2 0.8 fusion.14
  5.0 1.4 fusion.16
  6.4 0.2 fusion.4
  6.7 0.0 copy-done.4
  6.7 0.5 slice.32
  7.2 0.5 slice.31
  7.7 1.1 pad_maximum_fusion.part
  8.8 53.2 %gather.1.refs = bf16[32,2,9,64,128]{4,3,2,1,0:T(8,128)(2,1)S(1)} custom-call(bf16[2,9,64,128]{3,2,1,0:T(8,128)(2,1)S(1)} %fusion.2.own), custom_call_target="tpu_custom_call" | custom-call | tf_op jit(solution)/shard_map/gather/pallas_call | solution.py:488
  62.0 0.0 copy-start
  62.0 3.6 %copy-done = bf16[32,2,9,64,128]{4,3,2,1,0:T(8,128)(2,1)} copy-done((bf16[32,2,9,64,128]{4,3,2,1,0:T(8,128)(2,1)}, bf16[32,2,9,64,128]{4,3,2,1,0:T(8,128)(2,1)S(1)}, u32[]{:S(2)}) %copy-start) | copy-done | bytes 9437208
  65.6 0.0 copy-start.1
  65.6 0.0 copy-start.2
  65.6 0.0 copy-start.3
  65.6 100.7 %transform.1.wt = bf16[288,208,256]{2,1,0:T(8,128)(2,1)} custom-call(s32[8,2]{1,0:T(8,128)} %copy.23.shift, bf16[8,2,288,128]{3,2,1,0:T(8,128)(2,1)} %pad_maximum_fusion.part, f32[8,128]{1,0:T(8,128)} %select_reduce_fusion.ctf, f32[11,2,288,128]{3,2,1,0:T(8,128)} %constant.40.clone.tx, f32[11,2,288,128]{3,2,1,0:T(8,128)} %constant.41.clone.ty, ...), custom_call_target="tpu_custom_call" | custom-call | tf_op jit(solution)/shard_map/transform/pallas_call | solution.py:144
  166.2 0.0 copy-done.1
  166.2 0.0 copy-done.2
  166.2 0.0 copy-done.3
  166.3 39.1 %match.1 = (f32[19,208,128]{2,1,0:T(8,128)S(1)}, f32[8,128]{1,0:T(8,128)S(1)}, f32[8,128]{1,0:T(8,128)S(1)}, f32[8,128]{1,0:T(8,128)S(1)}) custom-call(bf16[288,208,256]{2,1,0:T(8,128)(2,1)} %transform.1.wt, bf16[32,2,9,64,128]{4,3,2,1,0:T(8,128)(2,1)} %copy-done, f32[8,128]{1,0:T(8,128)S(1)} %copy-done.3, f32[19,19,128]{2,1,0:T(8,128)S(1)} %copy-done.2, ...), custom_call_target="tpu_custom_call" | custom-call | tf_op jit(solution)/shard_map/match/pallas_call | solution.py:249
  205.4 0.1 slice_reduce_fusion
  205.5 0.1 slice_reduce_fusion.1
  205.6 8.9 %pmax.7 = f32[8]{0:T(128)S(1)} all-reduce(f32[8]{0:T(128)S(1)} %slice_reduce_fusion.1), channel_id=1, replica_groups=mesh['dp'=32,'cls'=4] {'cls'}, use_global_device_ids=true, to_apply=%region_1.2 | all-reduce | flops 8 | bytes 64 | tf_op jit(solution)/shard_map/pmax | solution.py:720
  214.5 8.1 %psum.7 = f32[8]{0:T(128)S(1)} all-reduce(f32[8]{0:T(128)S(1)} %exponential_multiply_fusion), channel_id=1, replica_groups=mesh['dp'=32,'cls'=4] {'cls'}, use_global_device_ids=true, to_apply=%region_2.3 | all-reduce | flops 8 | bytes 64 | tf_op jit(solution)/shard_map/psum | solution.py:721
  222.6 0.0 copy-start.5
  222.6 0.1 subtract_exponential_fusion.scale
  222.7 28.9 %back.1.own = bf16[32,2,9,64,128]{4,3,2,1,0:T(8,128)(2,1)} custom-call(bf16[288,208,256]{2,1,0:T(8,128)(2,1)} %transform.1.wt, f32[19,208,128]{2,1,0:T(8,128)S(1)} %get-tuple-element.10.spec, f32[8,128]{1,0:T(8,128)S(1)} %subtract_exponential_fusion.scale), custom_call_target="tpu_custom_call" | custom-call | tf_op jit(solution)/shard_map/back/pallas_call | solution.py:290
  251.6 0.0 copy-done.5
  251.6 61.6 %scatter.1 = f32[2,9,64,128]{3,2,1,0:T(8,128)S(1)} custom-call(bf16[32,2,9,64,128]{4,3,2,1,0:T(8,128)(2,1)} %back.1.own), custom_call_target="tpu_custom_call" | custom-call | tf_op jit(solution)/shard_map/scatter/pallas_call | solution.py:693
  313.2 0.2 fusion.7
  313.4 0.6 slice_multiply_fusion
  314.0 0.1 pad_maximum_fusion.1
  314.1 1.0 copy.26
  (4 shorter events, 0.1 us)
Async XLA Ops:
  0.6 6.1 %copy-start.4 = (bf16[8,2,288,128]{3,2,1,0:T(8,128)(2,1)S(1)}, bf16[8,2,288,128]{3,2,1,0:T(8,128)(2,1)}, u32[]{:S(2)}) copy-start(bf16[8,2,288,128]{3,2,1,0:T(8,128)(2,1)} %param.12) | copy-start | bytes 3538948
  62.0 3.6 %copy-start = (bf16[32,2,9,64,128]{4,3,2,1,0:T(8,128)(2,1)}, bf16[32,2,9,64,128]{4,3,2,1,0:T(8,128)(2,1)S(1)}, u32[]{:S(2)}) copy-start(bf16[32,2,9,64,128]{4,3,2,1,0:T(8,128)(2,1)S(1)} %gather.1.refs) | copy-start | bytes 28311556
  65.6 100.7 %copy-start.1 = (f32[19,19,128]{2,1,0:T(8,128)S(1)}, f32[19,19,128]{2,1,0:T(8,128)}, u32[]{:S(2)}) copy-start(f32[19,19,128]{2,1,0:T(8,128)} %constant.45.clone.bwd) | copy-start | bytes 554500
  65.6 100.7 %copy-start.2 = (f32[19,19,128]{2,1,0:T(8,128)S(1)}, f32[19,19,128]{2,1,0:T(8,128)}, u32[]{:S(2)}) copy-start(f32[19,19,128]{2,1,0:T(8,128)} %constant.44.clone.fwd) | copy-start | bytes 554500
  65.6 100.7 %copy-start.3 = (f32[8,128]{1,0:T(8,128)S(1)}, f32[8,128]{1,0:T(8,128)}, u32[]{:S(2)}) copy-start(f32[8,128]{1,0:T(8,128)} %select_reduce_fusion.ctf) | copy-start | bytes 12292
  222.6 28.9 %copy-start.5 = (f32[8]{0:T(128)}, f32[8]{0:T(128)S(1)}, u32[]{:S(2)}) copy-start(f32[8]{0:T(128)S(1)} %log_add_fusion) | copy-start | bytes 100

commit v2 on v1

v2 whole, which is shorter than its diff:
```python
import functools
import heapq
import math

import jax
import jax.numpy as jnp
import numpy as np
from jax import lax
from jax.experimental import pallas as pl
from jax.experimental.pallas import tpu as pltpu
from jax.sharding import PartitionSpec as P

ROTS = 36
SIDE = 5
SHIFTS = SIDE * SIDE
ANGLES = 288
CYCLES = 128
HALF = ANGLES // 2
REACH = 10
FOLD = ROTS // 2 + 1
IPAD = 80
QROWS = 208
CPAD = 64
F32 = jnp.float32
BF16 = jnp.bfloat16
MESH = pl.DeviceIdType.MESH


def phase_tables():
    order = np.concatenate([np.arange(0, ANGLES, 2), np.arange(1, ANGLES, 2)])
    theta = 2.0 * np.pi * order / ANGLES
    radius = (np.arange(CYCLES) + 1) / (2.0 * CYCLES)
    count = np.arange(REACH + 1)
    out = []
    for wave in (np.cos(theta), np.sin(theta)):
        arg = 2.0 * np.pi * count[:, None, None] * wave[None, :, None] * radius[None, None, :]
        out.append(np.stack([np.cos(arg), np.sin(arg)], 1).astype(np.float32))
    return out


def dft_tables():
    row = np.arange(IPAD)
    out = []
    for start in (0, 1):
        t = np.arange(start, ANGLES, 2)
        ang = 2.0 * np.pi * ((row[:, None] * t[None, :]) % ANGLES) / ANGLES
        out.append(np.concatenate([np.cos(ang), np.sin(ang)], 0).astype(np.float32))
    return out


def rotation_coefs():
    k = np.arange(FOLD)
    ang = 2.0 * np.pi * ((k[:, None] * k[None, :]) % ROTS) / ROTS
    cos, sin = np.cos(ang), np.sin(ang)
    lanes = np.arange(128) < CPAD
    fwd = np.where(lanes, cos[:, :, None], -sin[:, :, None]) / ANGLES
    bwd = np.where(lanes, cos[:, :, None], sin[:, :, None])
    return fwd.astype(np.float32), bwd.astype(np.float32)


SIZES = (4, 2, 4)
SUB = (5, 4)
LATE = 0.5


def place():
    dp = lax.axis_index("dp")
    return dp % 4, (dp // 4) % 2, dp // 8, lax.axis_index("cls")


def peer(me, rel):
    x, y, z, cls = me
    return ((((z + rel[2]) % 4) * 2 + (y + rel[1]) % 2) * 4 + (x + rel[0]) % 4, cls)


def slot(me, rel):
    return peer(me, rel)[0]


def toward(axis, sign):
    move = [0, 0, 0]
    move[axis] = sign
    return tuple(move)


def greet(me):
    barrier = pltpu.get_barrier_semaphore()
    moves = [toward(0, 1), toward(0, -1), toward(1, 1), toward(2, 1), toward(2, -1)]
    for move in moves:
        pl.semaphore_signal(barrier, inc=1, device_id=peer(me, move), device_id_type=MESH)
    pl.semaphore_wait(barrier, len(moves))


def axes_of(half):
    return (0, 1, 2) if half == 0 else (2, 1, 0)


def span(sub):
    return pl.ds(0, sum(SUB)) if sub is None else pl.ds(0 if sub == 0 else SUB[0], SUB[sub])


class Links:
    def __init__(self):
        self.free, self.heap, self.count = {}, [], 0

    def send(self, t, axis, sign, size, key):
        start = max(t, self.free.get((axis, sign), 0.0))
        self.free[(axis, sign)] = start + size
        self.push(start + size + LATE, key)

    def push(self, t, key):
        self.count += 1
        heapq.heappush(self.heap, (t, self.count, key))

    def pop(self):
        t, _, key = heapq.heappop(self.heap)
        return t, key


def gather_plan():
    links, plan, got = Links(), [], {}
    for half in (0, 1):
        links.push(0.0, (half, (0, 0, 0), None))
    while links.heap:
        t, key = links.pop()
        half, rel, sub = key
        order = axes_of(half)
        sends = []

        def go(axis, sign, sub):
            seen = list(rel)
            seen[axis] = (seen[axis] - sign) % SIZES[axis]
            there = (half, tuple(seen), sub)
            sends.append((half, rel, sub, axis, sign, there))
            links.send(t, axis, sign, 1.0 if sub is None else SUB[sub] / sum(SUB), there)

        got[half, rel] = got.get((half, rel), 0) + 1
        if sub is None or got[half, rel] == 2:
            last = max([i for i in range(3) if rel[order[i]]], default=-1)
            for i in range(2, last, -1):
                if order[i] == 1:
                    go(1, 1, None)
                else:
                    go(order[i], 1, None)
                    go(order[i], -1, None)
            if last >= 0 and order[last] != 1:
                if rel[order[last]] == 3:
                    go(order[last], 1, 0)
                elif rel[order[last]] == 1:
                    go(order[last], -1, 1)
        plan.append((t, None if rel == (0, 0, 0) else key, sends))
    return plan


def gather_keys():
    plan = gather_plan()
    recv = {step[1]: i for i, step in enumerate(s for s in plan if s[1] is not None)}
    return plan, recv


class Gather:
    def __init__(self, me, own, store, send_sem, recv_sem):
        self.me, self.own, self.store = me, own, store
        self.send_sem, self.recv_sem = send_sem, recv_sem
        self.plan, self.recv = gather_keys()
        self.sent = []

    def copy(self, index, half, rel, sub, axis, sign, there):
        where = span(sub)
        here = self.own.at[half, where] if rel == (0, 0, 0) else self.store.at[slot(self.me, rel), half, where]
        return pltpu.make_async_remote_copy(
            src_ref=here,
            dst_ref=self.store.at[slot(self.me, rel), half, where],
            send_sem=self.send_sem.at[index],
            recv_sem=self.recv_sem.at[self.recv[there]],
            device_id=peer(self.me, toward(axis, sign)),
            device_id_type=MESH,
        )

    def arrived(self, key):
        half, rel, sub = key
        here = self.store.at[slot(self.me, rel), half, span(sub)]
        pltpu.make_async_remote_copy(
            src_ref=here,
            dst_ref=here,
            send_sem=self.send_sem.at[0],
            recv_sem=self.recv_sem.at[self.recv[key]],
            device_id=peer(self.me, (1, 0, 0)),
            device_id_type=MESH,
        ).wait_recv()

    def step(self, item):
        _, key, sends = item
        if key is not None:
            self.arrived(key)
        for send in sends:
            self.copy(len(self.sent), *send).start()
            self.sent.append(send)

    def finish(self):
        for index, send in enumerate(self.sent):
            self.copy(index, *send).wait_send()


GROUP = 8
STEPS = 26
PITCH = 4 * IPAD + 1
UNIT_STEPS = 2.06


def transform_kernel(shift, part, ctf, tx, ty, te, to, own, out, store, z1, xs, fr, fi, send_sem, recv_sem, own_sem):
    u = pl.program_id(0)
    me = place()
    work = Gather(me, own, store, send_sem, recv_sem)
    keep = pltpu.make_async_copy(own, store.at[slot(me, (0, 0, 0))], own_sem)
    due = {}
    for item in work.plan:
        at = 0 if item[1] is None else min(STEPS - 1, math.ceil(item[0] * UNIT_STEPS))
        due.setdefault(at, []).append(item)

    @pl.when(u == 0)
    def _():
        greet(me)
        keep.start()

    for at in sorted(due):
        if at < STEPS - 1:

            @pl.when(u == at)
            def _(at=at):
                for item in due[at]:
                    work.step(item)

    s = jnp.minimum(u, SHIFTS - 1)
    a = s // SIDE
    b = s % SIDE

    @pl.when((b == 0) & (u < SHIFTS))
    def _():
        def ramp(p, carry):
            sx = shift[p, 0] + a - SIDE // 2
            n = jnp.abs(sx)
            sg = jnp.where(sx < 0, -1.0, 1.0).astype(F32)
            for c in range(0, ANGLES, 48):
                rows = pl.ds(c, 48)
                re = part[p, 0, rows, :].astype(F32)
                im = part[p, 1, rows, :].astype(F32)
                co = tx[n, 0, rows, :]
                si = tx[n, 1, rows, :] * sg
                z1[p, 0, rows, :] = re * co + im * si
                z1[p, 1, rows, :] = im * co - re * si
            return carry

        lax.fori_loop(0, GROUP, ramp, 0)

    @pl.when(u < SHIFTS)
    def _():
        for p in range(GROUP):
            sy = shift[p, 1] + b - SIDE // 2
            n = jnp.abs(sy)
            sg = jnp.where(sy < 0, -1.0, 1.0).astype(F32)
            for c in range(0, ANGLES, 16):
                rows = pl.ds(c, 16)
                re = z1[p, 0, rows, :]
                im = z1[p, 1, rows, :]
                co = ty[n, 0, rows, :]
                si = ty[n, 1, rows, :] * sg
                xs[rows, 256 * p : 256 * p + 128] = (re * co + im * si).astype(BF16)
                xs[rows, 256 * p + 128 : 256 * p + 256] = (im * co - re * si).astype(BF16)
        even = jnp.dot(te[...], xs[0:HALF, :], preferred_element_type=F32)
        odd = jnp.dot(to[...], xs[HALF:, :], preferred_element_type=F32)
        for p in range(GROUP):
            j = (u % 2) * GROUP + p
            gain = ctf[p : p + 1, :]
            lo, hi = slice(256 * p, 256 * p + 128), slice(256 * p + 128, 256 * p + 256)
            for c in range(0, IPAD, 8):
                cos, sin = slice(c, c + 8), slice(IPAD + c, IPAD + c + 8)
                u1 = (even[cos, lo] + even[sin, hi]) * gain
                u2 = (even[cos, lo] - even[sin, hi]) * gain
                w1 = (even[cos, hi] - even[sin, lo]) * gain
                w2 = (even[cos, hi] + even[sin, lo]) * gain
                v1 = (odd[cos, lo] + odd[sin, hi]) * gain
                v2 = (odd[cos, lo] - odd[sin, hi]) * gain
                y1 = (odd[cos, hi] - odd[sin, lo]) * gain
                y2 = (odd[cos, hi] + odd[sin, lo]) * gain
                for blk, (re, im) in enumerate(
                    ((u1 + v1, w1 + y1), (u1 - v1, w1 - y1), (u2 - v2, w2 - y2), (u2 + v2, w2 + y2))
                ):
                    rows = pl.ds(j * PITCH + blk * IPAD + c, 8)
                    fr[rows, :] = re
                    fi[rows, :] = im

    def emit(i, blk, m):
        rows = pl.ds(blk * IPAD + i, 2 * GROUP, stride=PITCH)
        out[m, :, 0:128] = fr[rows, :].astype(BF16)
        out[m, :, 128:256] = fi[rows, :].astype(BF16)

    @pl.when(u % 2 == 1)
    def _():
        def pack(i, carry):
            emit(i, 0, i)
            emit(i, 1, HALF + i)
            emit(i, 2, HALF - i)
            emit(i, 3, ANGLES - i)
            return carry

        emit(0, 0, 0)
        emit(0, 1, HALF)
        emit(HALF // 2, 0, HALF // 2)
        emit(HALF // 2, 1, HALF + HALF // 2)
        lax.fori_loop(1, HALF // 2, pack, 0, unroll=8)

    @pl.when(u == STEPS - 1)
    def _():
        for item in due.get(STEPS - 1, []):
            work.step(item)
        keep.wait()
        work.finish()


def transform(shift, part, ctf, own):
    tx, ty = phase_tables()
    te, to = dft_tables()
    plan, recv = gather_keys()
    whole = pl.BlockSpec(memory_space=pltpu.VMEM)
    owners = SIZES[0] * SIZES[1] * SIZES[2]
    return pl.pallas_call(
        transform_kernel,
        grid=(STEPS,),
        out_shape=(
            jax.ShapeDtypeStruct((ANGLES, QROWS, 256), BF16),
            jax.ShapeDtypeStruct((owners,) + own.shape, own.dtype),
        ),
        in_specs=[pl.BlockSpec(memory_space=pltpu.SMEM)] + [whole] * 7,
        out_specs=(
            pl.BlockSpec((ANGLES, 2 * GROUP, 256), lambda u: (0, u // 2, 0)),
            pl.BlockSpec(memory_space=pl.ANY),
        ),
        scratch_shapes=[
            pltpu.VMEM((GROUP, 2, ANGLES, 128), F32),
            pltpu.VMEM((ANGLES, 256 * GROUP), BF16),
            pltpu.VMEM((2 * GROUP * PITCH + 8, 128), F32),
            pltpu.VMEM((2 * GROUP * PITCH + 8, 128), F32),
            pltpu.SemaphoreType.DMA((sum(len(s[2]) for s in plan),)),
            pltpu.SemaphoreType.DMA((len(recv),)),
            pltpu.SemaphoreType.DMA,
        ],
        compiler_params=pltpu.CompilerParams(
            collective_id=1, has_side_effects=True, vmem_limit_bytes=56 * 2**20
        ),
        name="transform",
    )(shift, part, ctf, jnp.asarray(tx), jnp.asarray(ty), jnp.asarray(te, BF16), jnp.asarray(to, BF16), own)


H = FOLD // 2

def fold_of(r):
    return (r, 1) if r <= ROTS // 2 else (ROTS - r, -1)

def swap(t):
    return jnp.concatenate([t[:, CPAD:], t[:, :CPAD]], 1)

def half_sums(parts, tab, k):
    even = parts[0] * tab[k, 0:1, :]
    for g in range(2, FOLD, 2):
        even = even + parts[g] * tab[k, g : g + 1, :]
    odd = parts[1] * tab[k, 1:2, :]
    for g in range(3, FOLD, 2):
        odd = odd + parts[g] * tab[k, g : g + 1, :]
    return even, odd

def match_kernel(classes, wt, refs, ctf, fwd, bwd, spec, peak, mass, post, acc, power):
    d = pl.program_id(0)
    first = d == 0
    lanes = lax.broadcasted_iota(jnp.int32, (128, 128), 1)
    minus_high = jnp.where(lanes < CPAD, 1.0, -1.0).astype(BF16)

    def image(r):
        return jnp.concatenate([refs[r // 9, 0, r % 9], refs[r // 9, 1, r % 9]], 0)

    def product(r):
        t = image(r)
        if fold_of(r)[1] > 0:
            table = jnp.concatenate([t * minus_high, swap(t)], 0)
        else:
            table = jnp.concatenate([t, swap(t) * minus_high], 0)
        return jnp.dot(wt[r], table, preferred_element_type=F32)

    @pl.when(first)
    def _():
        acc[...] = jnp.zeros_like(acc)
        power[...] = jnp.zeros_like(power)

    for g in range(FOLD):
        y = product(g)
        if 0 < g < FOLD - 1:
            y = y + product(ROTS - g)
        acc[g] += y
    pw = power[...]
    for r in range(ROTS):
        tf = image(r).astype(F32)
        pw = pw + tf * tf
    power[...] = pw

    @pl.when(d == pl.num_programs(0) - 1)
    def _():
        gain = ctf[...]
        half = jnp.dot(
            gain * gain, power[...], precision=lax.Precision.HIGHEST, preferred_element_type=F32
        ) * (0.5 / ANGLES)
        bias = half + pltpu.roll(half, CPAD, 1)
        lane = lax.broadcasted_iota(jnp.int32, (8, 128), 1)
        live = lane % CPAD < classes
        edge = lane < classes
        sign = jnp.where(lane < CPAD, 1.0, -1.0).astype(F32)
        low = -1e30

        def score(s, top):
            rows = pl.ds(pl.multiple_of(s * 8, 8), 8)
            parts = [acc[g, rows, :] for g in range(FOLD)]
            for k in range(H + 1):
                even, odd = half_sums(parts, fwd, k)
                y, w = even + odd, even - odd
                both = [(k, y * sign + pltpu.roll(y, CPAD, 1))]
                if k < H:
                    both.append((FOLD - 1 - k, w + pltpu.roll(w * sign, CPAD, 1)))
                for at, z in both:
                    z = z - bias
                    z = jnp.where(edge if at in (0, FOLD - 1) else live, z, low)
                    spec[at, rows, :] = z
                    top = jnp.maximum(top, z)
            return top

        top = lax.fori_loop(0, SHIFTS, score, jnp.full((8, 128), low, F32))
        top = jnp.max(top, axis=1, keepdims=True)

        def weigh(s, total):
            rows = pl.ds(pl.multiple_of(s * 8, 8), 8)
            parts = []
            for k in range(FOLD):
                e = jnp.exp(spec[k, rows, :] - top)
                total = total + e
                parts.append(e * sign + pltpu.roll(e, CPAD, 1))
            for g in range(H + 1):
                even, odd = half_sums(parts, bwd, g)
                spec[g, rows, :] = even + odd
                if g < H:
                    spec[FOLD - 1 - g, rows, :] = (even - odd) * sign
            return total

        total = lax.fori_loop(0, SHIFTS, weigh, jnp.zeros((8, 128), F32))
        spec[:, SHIFTS * 8 :, :] = jnp.zeros((FOLD, QROWS - SHIFTS * 8, 128), F32)
        peak[...] = jnp.broadcast_to(top, (8, 128))
        mass[...] = jnp.broadcast_to(jnp.sum(total, axis=1, keepdims=True), (8, 128))
        post[...] = total + pltpu.roll(total, CPAD, 1)

def match(wt, refs, ctf, classes):
    fwd, bwd = rotation_coefs()
    small = jax.ShapeDtypeStruct((8, 128), F32)
    whole = pl.BlockSpec(memory_space=pltpu.VMEM)
    return pl.pallas_call(
        functools.partial(match_kernel, classes),
        grid=(ANGLES // ROTS,),
        out_shape=(jax.ShapeDtypeStruct((FOLD, QROWS, 128), F32), small, small, small),
        in_specs=[pl.BlockSpec((ROTS, QROWS, 256), lambda d: (d, 0, 0)),
                  pl.BlockSpec((4, 2, 9, CPAD, 128), lambda d: (d, 0, 0, 0, 0)), whole, whole, whole],
        out_specs=(whole,) * 4,
        scratch_shapes=[pltpu.VMEM((FOLD, QROWS, 128), F32), pltpu.VMEM((128, 128), F32)],
        compiler_params=pltpu.CompilerParams(vmem_limit_bytes=48 * 2**20),
        name="match",
    )(wt, refs, ctf, jnp.asarray(fwd), jnp.asarray(bwd))

COMBOS = [(ry, c) for ry in (1, 0) for c in (2, 1, 3, 0)]
BLOCKS = [(2, 1), (2, 0), (1, 1), (3, 1), (1, 0), (3, 0), (0, 1), (0, 0)]
BLOCK_UNITS = 0.6


def scatter_plan():
    links, steps, got, done = Links(), [], set(), set()

    def send(t, half, stage, combo, kind):
        axis = axes_of(half)[::-1][stage]
        sign = 1 if kind in ("a0", "l0", "l1", "y") else -1
        size = 1.0 if kind == "y" else SUB[int(kind[1])] / sum(SUB)
        msg = (half, stage, combo, kind)
        steps.append((t, "send", msg))
        links.send(t, axis, sign, size, msg)

    def have(half, stage, combo, k):
        if stage == 2:
            return (half, 2, k) in done
        return ((k, combo[0]) if half == 0 else (combo[1], combo[0])) in done

    def ready(t, half, stage, combo, k):
        if k == 2:
            send(t, half, stage, combo, "a0")
            send(t, half, stage, combo, "a1")
        elif k == 1:
            send(t, half, stage, combo, "l1")
            relay(t, half, stage, combo, "a0")
        elif k == 3:
            send(t, half, stage, combo, "r0")
            relay(t, half, stage, combo, "a1")
        else:
            total(t, half, stage, combo)

    def relay(t, half, stage, combo, kind):
        k = 1 if kind == "a0" else 3
        if (half, stage, combo, kind) in got and have(half, stage, combo, k):
            steps.append((t, "relay", (half, stage, combo, kind)))
            send(t, half, stage, combo, "l0" if kind == "a0" else "r1")

    def total(t, half, stage, combo):
        kinds = ("l0", "l1", "r0", "r1")
        if all((half, stage, combo, kind) in got for kind in kinds) and have(half, stage, combo, 0):
            steps.append((t, "total", (half, stage, combo)))
            if stage == 0:
                done.add((half, 0, combo, "s"))
                if combo[0] == 1:
                    send(t, half, 1, combo[1], "y")
                else:
                    second(t, half, combo[1])

    def second(t, half, c):
        if (half, 0, (0, c), "s") in done and (half, 1, c, "y") in got:
            steps.append((t, "pair", (half, c)))
            done.add((half, 2, c))
            ready(t, half, 2, None, c)

    for i, block in enumerate(BLOCKS):
        links.push((i + 1) * BLOCK_UNITS, ("block", block))
    while links.heap:
        t, key = links.pop()
        if key[0] == "block":
            z, y = key[1]
            done.add((z, y))
            for x in (2, 1, 3, 0):
                ready(t, 0, 0, (y, x), z)
                ready(t, 1, 0, (y, z), x)
            continue
        half, stage, combo, kind = key
        steps.append((t, "wait", key))
        got.add(key)
        if kind == "y":
            second(t, half, combo)
        elif kind in ("a0", "a1"):
            relay(t, half, stage, combo, kind)
        else:
            total(t, half, stage, combo)
    return steps


def scatter_keys():
    steps = scatter_plan()
    return steps, {s[2]: i for i, s in enumerate(s for s in steps if s[1] == "send")}


class Scatter:
    def __init__(self, me, own, three, pair, out, send_sem, recv_sem):
        self.me, self.own, self.three, self.pair, self.out = me, own, three, pair, out
        self.send_sem, self.recv_sem = send_sem, recv_sem
        self.steps, self.index = scatter_keys()
        self.sent = []

    def group(self, stage, combo):
        return 8 if stage == 2 else COMBOS.index(combo)

    def mine(self, half, stage, combo, k):
        if stage == 2:
            return self.pair.at[half, k]
        order = axes_of(half)[::-1]
        rel = [0, 0, 0]
        rel[order[0]] = k
        rel[1] = combo[0]
        rel[order[2]] = combo[1]
        return self.own.at[slot(self.me, rel), half]

    def box(self, msg):
        half, stage, combo, kind = msg
        if kind == "y":
            return self.pair.at[half, combo]
        which = {"a": 0, "l": 1, "r": 2}[kind[0]]
        return self.three.at[half, self.group(stage, combo), which, span(int(kind[1]))]

    def source(self, msg):
        half, stage, combo, kind = msg
        if kind == "y":
            return self.three.at[half, self.group(0, (1, combo)), 1]
        where = span(int(kind[1]))
        if kind in ("a0", "a1"):
            return self.mine(half, stage, combo, 2).at[where]
        if kind == "l1":
            return self.mine(half, stage, combo, 1).at[where]
        if kind == "r0":
            return self.mine(half, stage, combo, 3).at[where]
        return self.three.at[half, self.group(stage, combo), 0, where]

    def copy(self, msg, src=None):
        half, stage, combo, kind = msg
        axis = axes_of(half)[::-1][stage]
        sign = 1 if kind in ("a0", "l0", "l1", "y") else -1
        i = self.index[msg]
        box = self.box(msg)
        return pltpu.make_async_remote_copy(
            src_ref=box if src is None else src,
            dst_ref=box,
            send_sem=self.send_sem.at[i],
            recv_sem=self.recv_sem.at[i],
            device_id=peer(self.me, toward(axis, sign)),
            device_id_type=MESH,
        )

    def add(self, dst, terms, count):
        def one(i, carry):
            value = terms[0][i].astype(F32)
            for term in terms[1:]:
                value = value + term[i].astype(F32)
            dst[i] = value.astype(dst.dtype)
            return carry

        lax.fori_loop(0, count, one, 0)

    def step(self, item):
        _, what, key = item
        if what == "send":
            self.copy(key, self.source(key)).start()
            self.sent.append(key)
        elif what == "wait":
            self.copy(key).wait_recv()
        elif what == "relay":
            half, stage, combo, kind = key
            box = self.box(key)
            mine = self.mine(half, stage, combo, 1 if kind == "a0" else 3).at[span(int(kind[1]))]
            self.add(box, (mine, box), SUB[int(kind[1])])
        elif what == "pair":
            half, c = key
            box = self.pair.at[half, c]
            self.add(box, (self.three.at[half, self.group(0, (0, c)), 1], box), sum(SUB))
        else:
            half, stage, combo = key
            left = self.three.at[half, self.group(stage, combo), 1]
            right = self.three.at[half, self.group(stage, combo), 2]
            mine = self.mine(half, stage, combo, 0)
            dst = self.out.at[half] if stage == 2 else left
            self.add(dst, (mine, left, right), sum(SUB))

    def finish(self):
        for key in self.sent:
            self.copy(key, self.source(key)).wait_send()


def back_kernel(wt, spec, stat, out, logz, own, three, pair, tab, seen, send_sem, recv_sem, stat_send, stat_recv):
    i = pl.program_id(0)
    me = place()
    x, y, z, cls = me
    work = Scatter(me, own, three, pair, out, send_sem, recv_sem)
    last = len(BLOCKS) - 1
    due = {}
    for item in work.steps:
        at = min(last, max(0, math.ceil(item[0] / BLOCK_UNITS - 0.001) - 1))
        due.setdefault(at, []).append(item)

    @pl.when(i == 0)
    def _():
        dp = slot(me, (0, 0, 0))
        barrier = pltpu.get_barrier_semaphore()
        there = [peer(me, toward(*move)) for move in ((0, 1), (0, -1), (1, 1), (2, 1), (2, -1))]
        others = [(dp, (cls + k) % 4) for k in (1, 2, 3)]
        for device in there + others:
            pl.semaphore_signal(barrier, inc=1, device_id=device, device_id_type=MESH)
        pl.semaphore_wait(barrier, len(there) + len(others))
        copies = []
        for k, device in enumerate(others):
            copy = pltpu.make_async_remote_copy(
                src_ref=stat,
                dst_ref=seen.at[k],
                send_sem=stat_send.at[k],
                recv_sem=stat_recv.at[k],
                device_id=device,
                device_id_type=MESH,
            )
            copy.start()
            copies.append(copy)
        for copy in copies:
            copy.wait()
        peaks = [stat[0]] + [seen[k, 0] for k in range(3)]
        masses = [stat[1]] + [seen[k, 1] for k in range(3)]
        top = jnp.maximum(jnp.maximum(peaks[0], peaks[1]), jnp.maximum(peaks[2], peaks[3]))
        mass = masses[0] * jnp.exp(peaks[0] - top)
        for k in range(1, 4):
            mass = mass + masses[k] * jnp.exp(peaks[k] - top)
        total = top + jnp.log(mass)
        logz[...] = total
        scale = jnp.concatenate([jnp.exp(peaks[0] - total)] * (QROWS // 8), 0)
        for g in range(FOLD):
            tab[g] = (spec[g] * scale).T.astype(BF16)

    dz = jnp.int32(0)
    dy = jnp.int32(0)
    for at, (bz, by) in enumerate(BLOCKS):
        dz = jnp.where(i == at, bz, dz)
        dy = jnp.where(i == at, by, dy)
    base = (((z + dz) % 4) * 2 + (y + dy) % 2) * 4
    for r in range(ROTS):
        g, sg = fold_of(r)
        both = jnp.dot(tab[g], wt[r], preferred_element_type=F32)
        a, b = both[:CPAD], both[CPAD:]
        own[base + r // 9, 0, r % 9] = (a[:, :128] - sg * b[:, 128:]).astype(BF16)
        own[base + r // 9, 1, r % 9] = (a[:, 128:] + sg * b[:, :128]).astype(BF16)

    for at in range(len(BLOCKS)):

        @pl.when(i == at)
        def _(at=at):
            for item in due.get(at, []):
                work.step(item)
            if at == last:
                work.finish()


def block_index(i):
    dp = lax.axis_index("dp")
    dz = jnp.int32(0)
    dy = jnp.int32(0)
    for at, (bz, by) in enumerate(BLOCKS):
        dz = jnp.where(i == at, bz, dz)
        dy = jnp.where(i == at, by, dy)
    return ((dp // 8 + dz) % 4) * 2 + ((dp // 4) % 2 + dy) % 2, 0, 0


def back(wt, spec, stat):
    steps, index = scatter_keys()
    whole = pl.BlockSpec(memory_space=pltpu.VMEM)
    owners = SIZES[0] * SIZES[1] * SIZES[2]
    block = (ANGLES // owners, CPAD, 128)
    return pl.pallas_call(
        back_kernel,
        grid=(len(BLOCKS),),
        out_shape=(jax.ShapeDtypeStruct((2,) + block, F32), jax.ShapeDtypeStruct((8, 128), F32)),
        in_specs=[pl.BlockSpec((ROTS, QROWS, 256), block_index), whole, whole],
        out_specs=(whole, whole),
        scratch_shapes=[
            pltpu.VMEM((owners, 2) + block, BF16),
            pltpu.VMEM((2, 9, 3) + block, BF16),
            pltpu.VMEM((2, 4) + block, BF16),
            pltpu.VMEM((FOLD, 128, QROWS), BF16),
            pltpu.VMEM((3, 2, 8, 128), F32),
            pltpu.SemaphoreType.DMA((len(index),)),
            pltpu.SemaphoreType.DMA((len(index),)),
            pltpu.SemaphoreType.DMA((3,)),
            pltpu.SemaphoreType.DMA((3,)),
        ],
        compiler_params=pltpu.CompilerParams(
            collective_id=2, has_side_effects=True, vmem_limit_bytes=48 * 2**20
        ),
        name="back",
    )(wt, spec, stat)


def twist_tables(freq, rot_offset):
    idx = (freq[:, None] * rot_offset[None, :]) % ANGLES
    rad = idx.astype(F32) * (2.0 * math.pi / ANGLES)
    return jnp.cos(rad)[:, :, None], jnp.sin(rad)[:, :, None]


def twist_refs(references, cos, sin):
    re = references[:, 0].astype(F32)
    im = references[:, 1].astype(F32)
    both = jnp.stack([re * cos + im * sin, im * cos - re * sin], 1)
    both = jnp.pad(both, ((0, 0), (0, 0), (0, CPAD - both.shape[2]), (0, 0))).astype(BF16)
    both = both.reshape(both.shape[0], 2 * CPAD, 2, 64)
    return jnp.transpose(both, (2, 0, 3, 1))


def untwist(sums, cos, sin, classes):
    re = sums[0, :, :classes].astype(F32)
    im = sums[1, :, :classes].astype(F32)
    return jnp.stack([re * cos - im * sin, re * sin + im * cos], 1)


def order_angles(particles):
    return jnp.concatenate([particles[:, :, 0::2], particles[:, :, 1::2]], 2)


def group_rows(defocus_group, ctf_table):
    hit = defocus_group[:, None] == jnp.arange(ctf_table.shape[0], dtype=jnp.int32)[None, :]
    return jnp.sum(jnp.where(hit[:, :, None], ctf_table[None], 0.0), 1)


def local(particles, references, ctf_table, rot_offset, prior_shift, defocus_group):
    block, _, classes = references.shape[:3]
    freq = lax.axis_index("dp") * block + jnp.arange(block, dtype=jnp.int32)
    cos, sin = twist_tables(freq, rot_offset)
    ctf = group_rows(defocus_group, ctf_table)
    wt, refs = transform(prior_shift, order_angles(particles), ctf, twist_refs(references, cos, sin))
    spec, peak, mass, post = match(wt, refs, ctf, classes)
    sums, total = back(wt, spec, jnp.stack([peak, mass]))
    posterior = post[:, :classes] * jnp.exp(peak[:, :classes] - total[:, :classes])
    return total[:, 0], posterior, untwist(sums, cos, sin, classes)


def solution(mesh):
    placed = (
        P("dp", None, None, None),
        P("dp", None, "cls", None),
        P(),
        P("cls"),
        P("dp", None),
        P("dp"),
    )
    return jax.shard_map(
        local,
        mesh=mesh,
        in_specs=placed,
        out_specs=(P("dp"), P("dp", "cls"), P("dp", None, "cls", None)),
        check_vma=False,
    )
```

time: 317 us -> 162 us (0.51)
  Pallas kernels: 283 us -> 149 us
  blocking collectives: 17 us -> 0 us
    pallas_call x5 -> x3, Pallas kernels: 283 us -> 149 us  [the longest x1 63 us: transform(): pl.pallas_call(transform_kernel, grid=(STEPS,), out_shape=(jax.ShapeDtype...]
    pmax x1 -> x0, blocking collectives: 8.9 us -> none  [local(): top = lax.pmax(peak[:, 0], 'cls')]
    psum x1 -> x0, blocking collectives: 8.08 us -> none  [local(): lax.psum(mass[:, 0] * jnp.exp(peak[:, 0] - top), 'cls')]
    unnamed x14 -> x11, local copies, waits for them, and re-layouts: 5.94 us -> 2.39 us
where the time goes in v2:
time: 162 us
  Pallas kernels  149 us (92%)
  local copies, waits for them, and re-layouts  7.06 us (4%)
  other arithmetic  5.09 us (3%)
    pallas_call x1, Pallas kernels, transform(): pl.pallas_call(transform_kernel, grid=(STEPS,), out_shape=(jax.ShapeDtype...  63 us
    pallas_call x1, Pallas kernels, back(): pl.pallas_call(back_kernel, grid=(len(BLOCKS),), out_shape=(jax.ShapeDtyp...  61.6 us
    pallas_call x1, Pallas kernels, match(): pl.pallas_call(functools.partial(match_kernel, classes), grid=(ANGLES //...  24.5 us

profile of v2, /device:TPU:0, one launch (start us, length us, event | category | flops | bytes accessed | tf_op | source)
XLA Modules:
  0.0 162.1 jit_solution(4638408041598971804)
XLA Ops:
  0.6 0.7 iota_compare_fusion
  1.4 1.4 select_reduce_fusion.ctf
  2.8 1.3 copy.29.shift
  4.1 0.8 fusion.11
  4.9 0.0 copy-start.3
  4.9 1.6 fusion.13
  6.5 0.2 fusion.1
  6.8 0.3 reshape.140
  7.0 1.2 copy.28
  8.3 0.0 copy-done.3
  8.3 0.5 slice.31
  8.8 0.5 slice.30
  9.3 1.1 pad_maximum_fusion.part
  10.4 0.0 copy-start
  10.4 0.0 copy-start.1
  10.4 0.0 copy-start.2
  10.4 63.0 %transform.1 = (bf16[288,208,256]{2,1,0:T(8,128)(2,1)}, bf16[32,2,9,64,128]{4,3,2,1,0:T(8,128)(2,1)}) custom-call(s32[8,2]{1,0:T(8,128)} %copy.29.shift, bf16[8,2,288,128]{3,2,1,0:T(8,128)(2,1)} %pad_maximum_fusion.part, f32[8,128]{1,0:T(8,128)} %select_reduce_fusion.ctf, f32[11,2,288,128]{3,2,1,0:T(8,128)} %constant.40.clone.tx, ...), custom_call_target="tpu_custom_call" | custom-call | tf_op jit(solution)/shard_map/transform/pallas_call | solution.py:327
  73.4 0.0 copy-done
  73.4 0.0 copy-done.1
  73.4 0.0 copy-done.2
  73.4 24.5 %match.1 = (f32[19,208,128]{2,1,0:T(8,128)S(1)}, f32[8,128]{1,0:T(8,128)S(1)}, f32[8,128]{1,0:T(8,128)S(1)}, f32[8,128]{1,0:T(8,128)S(1)}) custom-call(bf16[288,208,256]{2,1,0:T(8,128)(2,1)} %get-tuple-element.11.wt, bf16[32,2,9,64,128]{4,3,2,1,0:T(8,128)(2,1)} %get-tuple-element.12.refs, f32[8,128]{1,0:T(8,128)S(1)} %copy-done.2, ...), custom_call_target="tpu_custom_call" | custom-call | tf_op jit(solution)/shard_map/match/pallas_call | solution.py:461
  97.9 61.6 %back.1 = (f32[2,9,64,128]{3,2,1,0:T(8,128)S(1)}, f32[8,128]{1,0:T(8,128)S(1)}) custom-call(bf16[288,208,256]{2,1,0:T(8,128)(2,1)} %get-tuple-element.11.wt, f32[19,208,128]{2,1,0:T(8,128)S(1)} %get-tuple-element.13.spec, f32[2,8,128]{2,1,0:T(8,128)S(1)} %pad_maximum_fusion.3.stat), custom_call_target="tpu_custom_call" | custom-call | tf_op jit(solution)/shard_map/back/pallas_call | solution.py:736
  159.6 0.6 exponential_multiply_fusion
  160.2 0.2 fusion.4
  160.4 0.1 pad_maximum_fusion.1
  160.4 1.0 copy.30
  161.5 0.6 slice_reduce_fusion
  (5 shorter events, 0.1 us)
Async XLA Ops:
  4.9 3.4 %copy-start.3 = (bf16[8,2,288,128]{3,2,1,0:T(8,128)(2,1)S(1)}, bf16[8,2,288,128]{3,2,1,0:T(8,128)(2,1)}, u32[]{:S(2)}) copy-start(bf16[8,2,288,128]{3,2,1,0:T(8,128)(2,1)} %param.12) | copy-start | bytes 3538948
  10.4 63.0 %copy-start = (f32[19,19,128]{2,1,0:T(8,128)S(1)}, f32[19,19,128]{2,1,0:T(8,128)}, u32[]{:S(2)}) copy-start(f32[19,19,128]{2,1,0:T(8,128)} %constant.45.clone.bwd) | copy-start | bytes 554500
  10.4 63.0 %copy-start.1 = (f32[19,19,128]{2,1,0:T(8,128)S(1)}, f32[19,19,128]{2,1,0:T(8,128)}, u32[]{:S(2)}) copy-start(f32[19,19,128]{2,1,0:T(8,128)} %constant.44.clone.fwd) | copy-start | bytes 554500
  10.4 63.0 %copy-start.2 = (f32[8,128]{1,0:T(8,128)S(1)}, f32[8,128]{1,0:T(8,128)}, u32[]{:S(2)}) copy-start(f32[8,128]{1,0:T(8,128)} %select_reduce_fusion.ctf) | copy-start | bytes 12292

commit v3 on v2

--- a/solution.py
+++ b/solution.py
@@ -59,8 +59,9 @@
 
 
 SIZES = (4, 2, 4)
-SUB = (5, 4)
-LATE = 0.5
+TILES = 57
+PARTS = ((0, 15, 29), (29, 43, 57))
+LATE = 0.35
 
 
 def place():
@@ -95,8 +96,15 @@
     return (0, 1, 2) if half == 0 else (2, 1, 0)
 
 
-def span(sub):
-    return pl.ds(0, sum(SUB)) if sub is None else pl.ds(0 if sub == 0 else SUB[0], SUB[sub])
+def span(half, sub):
+    low, mid, high = PARTS[half]
+    first, end = ((low, high), (low, mid), (mid, high))[0 if sub is None else sub + 1]
+    return pl.ds(first, end - first)
+
+
+def share(half, sub):
+    low, mid, high = PARTS[half]
+    return ((high - low) if sub is None else (mid - low, high - mid)[sub]) * 2.0 / TILES
 
 
 class Links:
@@ -132,7 +140,7 @@
             seen[axis] = (seen[axis] - sign) % SIZES[axis]
             there = (half, tuple(seen), sub)
             sends.append((half, rel, sub, axis, sign, there))
-            links.send(t, axis, sign, 1.0 if sub is None else SUB[sub] / sum(SUB), there)
+            links.send(t, axis, sign, share(half, sub), there)
 
         got[half, rel] = got.get((half, rel), 0) + 1
         if sub is None or got[half, rel] == 2:
@@ -166,11 +174,11 @@
         self.sent = []
 
     def copy(self, index, half, rel, sub, axis, sign, there):
-        where = span(sub)
-        here = self.own.at[half, where] if rel == (0, 0, 0) else self.store.at[slot(self.me, rel), half, where]
+        where = span(half, sub)
+        here = self.own.at[where] if rel == (0, 0, 0) else self.store.at[slot(self.me, rel), where]
         return pltpu.make_async_remote_copy(
             src_ref=here,
-            dst_ref=self.store.at[slot(self.me, rel), half, where],
+            dst_ref=self.store.at[slot(self.me, rel), where],
             send_sem=self.send_sem.at[index],
             recv_sem=self.recv_sem.at[self.recv[there]],
             device_id=peer(self.me, toward(axis, sign)),
@@ -179,7 +187,7 @@
 
     def arrived(self, key):
         half, rel, sub = key
-        here = self.store.at[slot(self.me, rel), half, span(sub)]
+        here = self.store.at[slot(self.me, rel), span(half, sub)]
         pltpu.make_async_remote_copy(
             src_ref=here,
             dst_ref=here,
@@ -208,7 +216,7 @@
 UNIT_STEPS = 2.06
 
 
-def transform_kernel(shift, part, ctf, tx, ty, te, to, own, out, store, z1, xs, fr, fi, send_sem, recv_sem, own_sem):
+def transform_kernel(shift, group, part, ctf, txh, tyh, te, to, own, out, store, tx, ty, z1, xs, fr, fi, send_sem, recv_sem, own_sem, tab_sem):
     u = pl.program_id(0)
     me = place()
     work = Gather(me, own, store, send_sem, recv_sem)
@@ -218,8 +226,12 @@
         at = 0 if item[1] is None else min(STEPS - 1, math.ceil(item[0] * UNIT_STEPS))
         due.setdefault(at, []).append(item)
 
+    loads = [pltpu.make_async_copy(txh, tx, tab_sem.at[0]), pltpu.make_async_copy(tyh, ty, tab_sem.at[1])]
+
     @pl.when(u == 0)
     def _():
+        for load in loads:
+            load.start()
         greet(me)
         keep.start()
 
@@ -230,6 +242,11 @@
             def _(at=at):
                 for item in due[at]:
                     work.step(item)
+
+    @pl.when(u == 0)
+    def _():
+        for load in loads:
+            load.wait()
 
     s = jnp.minimum(u, SHIFTS - 1)
     a = s // SIDE
@@ -271,7 +288,7 @@
         odd = jnp.dot(to[...], xs[HALF:, :], preferred_element_type=F32)
         for p in range(GROUP):
             j = (u % 2) * GROUP + p
-            gain = ctf[p : p + 1, :]
+            gain = ctf[pl.ds(group[p], 1), :]
             lo, hi = slice(256 * p, 256 * p + 128), slice(256 * p + 128, 256 * p + 256)
             for c in range(0, IPAD, 8):
                 cos, sin = slice(c, c + 8), slice(IPAD + c, IPAD + c + 8)
@@ -318,11 +335,13 @@
         work.finish()
 
 
-def transform(shift, part, ctf, own):
+def transform(shift, group, part, ctf, own):
     tx, ty = phase_tables()
     te, to = dft_tables()
     plan, recv = gather_keys()
     whole = pl.BlockSpec(memory_space=pltpu.VMEM)
+    near = pl.BlockSpec(memory_space=pltpu.SMEM)
+    far = pl.BlockSpec(memory_space=pl.ANY)
     owners = SIZES[0] * SIZES[1] * SIZES[2]
     return pl.pallas_call(
         transform_kernel,
@@ -331,12 +350,14 @@
             jax.ShapeDtypeStruct((ANGLES, QROWS, 256), BF16),
             jax.ShapeDtypeStruct((owners,) + own.shape, own.dtype),
         ),
-        in_specs=[pl.BlockSpec(memory_space=pltpu.SMEM)] + [whole] * 7,
+        in_specs=[near, near, whole, whole, far, far, whole, whole, whole],
         out_specs=(
             pl.BlockSpec((ANGLES, 2 * GROUP, 256), lambda u: (0, u // 2, 0)),
             pl.BlockSpec(memory_space=pl.ANY),
         ),
         scratch_shapes=[
+            pltpu.VMEM((REACH + 1, 2, ANGLES, 128), F32),
+            pltpu.VMEM((REACH + 1, 2, ANGLES, 128), F32),
             pltpu.VMEM((GROUP, 2, ANGLES, 128), F32),
             pltpu.VMEM((ANGLES, 256 * GROUP), BF16),
             pltpu.VMEM((2 * GROUP * PITCH + 8, 128), F32),
@@ -344,21 +365,20 @@
             pltpu.SemaphoreType.DMA((sum(len(s[2]) for s in plan),)),
             pltpu.SemaphoreType.DMA((len(recv),)),
             pltpu.SemaphoreType.DMA,
+            pltpu.SemaphoreType.DMA((2,)),
         ],
         compiler_params=pltpu.CompilerParams(
             collective_id=1, has_side_effects=True, vmem_limit_bytes=56 * 2**20
         ),
         name="transform",
-    )(shift, part, ctf, jnp.asarray(tx), jnp.asarray(ty), jnp.asarray(te, BF16), jnp.asarray(to, BF16), own)
+    )(shift, group, part, ctf, jnp.asarray(tx), jnp.asarray(ty), jnp.asarray(te, BF16), jnp.asarray(to, BF16), own)
 
 
 H = FOLD // 2
+HALF_ROWS = TILES * 8
 
 def fold_of(r):
     return (r, 1) if r <= ROTS // 2 else (ROTS - r, -1)
-
-def swap(t):
-    return jnp.concatenate([t[:, CPAD:], t[:, :CPAD]], 1)
 
 def half_sums(parts, tab, k):
     even = parts[0] * tab[k, 0:1, :]
@@ -369,46 +389,54 @@
         odd = odd + parts[g] * tab[k, g : g + 1, :]
     return even, odd
 
-def match_kernel(classes, wt, refs, ctf, fwd, bwd, spec, peak, mass, post, acc, power):
+def match_kernel(classes, group, wt, refs, ctf, fwd, bwd, spec, peak, mass, post, acc, power, flat):
     d = pl.program_id(0)
     first = d == 0
-    lanes = lax.broadcasted_iota(jnp.int32, (128, 128), 1)
-    minus_high = jnp.where(lanes < CPAD, 1.0, -1.0).astype(BF16)
-
-    def image(r):
-        return jnp.concatenate([refs[r // 9, 0, r % 9], refs[r // 9, 1, r % 9]], 0)
-
-    def product(r):
-        t = image(r)
+    for o in range(4):
+        flat[o, 0 : TILES * 16] = refs[o].reshape(TILES * 16, 128).astype(F32)
+
+    def image(r, part):
+        at = part * HALF_ROWS + (r % 9) * classes
+        return flat[r // 9, pl.ds(at, CPAD), :]
+
+    def product(r, squares):
+        re, im = image(r, 0), image(r, 1)
+        squares.append(re * re + im * im)
+        re, im = re.astype(BF16), im.astype(BF16)
         if fold_of(r)[1] > 0:
-            table = jnp.concatenate([t * minus_high, swap(t)], 0)
+            table = jnp.concatenate([jnp.concatenate([re, im], 1), jnp.concatenate([-im, re], 1)], 0)
         else:
-            table = jnp.concatenate([t, swap(t) * minus_high], 0)
-        return jnp.dot(wt[r], table, preferred_element_type=F32)
+            table = jnp.concatenate([jnp.concatenate([re, im], 1), jnp.concatenate([im, -re], 1)], 0)
+        return lax.dot_general(wt[r], table, (((1,), (1,)), ((), ())), preferred_element_type=F32)
 
     @pl.when(first)
     def _():
         acc[...] = jnp.zeros_like(acc)
         power[...] = jnp.zeros_like(power)
-
+        flat[:, TILES * 16 :] = jnp.zeros((4, 8, 128), F32)
+
+    pw = power[...]
     for g in range(FOLD):
-        y = product(g)
+        squares = []
+        y = product(g, squares)
         if 0 < g < FOLD - 1:
-            y = y + product(ROTS - g)
+            y = y + product(ROTS - g, squares)
         acc[g] += y
-    pw = power[...]
-    for r in range(ROTS):
-        tf = image(r).astype(F32)
-        pw = pw + tf * tf
+        for term in squares:
+            pw = pw + term
     power[...] = pw
 
     @pl.when(d == pl.num_programs(0) - 1)
     def _():
-        gain = ctf[...]
-        half = jnp.dot(
-            gain * gain, power[...], precision=lax.Precision.HIGHEST, preferred_element_type=F32
+        gain = jnp.concatenate([ctf[pl.ds(group[p], 1), :] for p in range(8)], 0)
+        half = lax.dot_general(
+            gain * gain,
+            power[...],
+            (((1,), (1,)), ((), ())),
+            precision=lax.Precision.HIGHEST,
+            preferred_element_type=F32,
         ) * (0.5 / ANGLES)
-        bias = half + pltpu.roll(half, CPAD, 1)
+        bias = jnp.concatenate([half, half], 1)
         lane = lax.broadcasted_iota(jnp.int32, (8, 128), 1)
         live = lane % CPAD < classes
         edge = lane < classes
@@ -431,7 +459,7 @@
                     top = jnp.maximum(top, z)
             return top
 
-        top = lax.fori_loop(0, SHIFTS, score, jnp.full((8, 128), low, F32))
+        top = lax.fori_loop(0, SHIFTS, score, jnp.full((8, 128), low, F32), unroll=5)
         top = jnp.max(top, axis=1, keepdims=True)
 
         def weigh(s, total):
@@ -448,13 +476,13 @@
                     spec[FOLD - 1 - g, rows, :] = (even - odd) * sign
             return total
 
-        total = lax.fori_loop(0, SHIFTS, weigh, jnp.zeros((8, 128), F32))
+        total = lax.fori_loop(0, SHIFTS, weigh, jnp.zeros((8, 128), F32), unroll=5)
         spec[:, SHIFTS * 8 :, :] = jnp.zeros((FOLD, QROWS - SHIFTS * 8, 128), F32)
         peak[...] = jnp.broadcast_to(top, (8, 128))
         mass[...] = jnp.broadcast_to(jnp.sum(total, axis=1, keepdims=True), (8, 128))
         post[...] = total + pltpu.roll(total, CPAD, 1)
 
-def match(wt, refs, ctf, classes):
+def match(group, wt, refs, ctf, classes):
     fwd, bwd = rotation_coefs()
     small = jax.ShapeDtypeStruct((8, 128), F32)
     whole = pl.BlockSpec(memory_space=pltpu.VMEM)
@@ -462,13 +490,13 @@
         functools.partial(match_kernel, classes),
         grid=(ANGLES // ROTS,),
         out_shape=(jax.ShapeDtypeStruct((FOLD, QROWS, 128), F32), small, small, small),
-        in_specs=[pl.BlockSpec((ROTS, QROWS, 256), lambda d: (d, 0, 0)),
-                  pl.BlockSpec((4, 2, 9, CPAD, 128), lambda d: (d, 0, 0, 0, 0)), whole, whole, whole],
+        in_specs=[pl.BlockSpec(memory_space=pltpu.SMEM), pl.BlockSpec((ROTS, QROWS, 256), lambda d: (d, 0, 0)),
+                  pl.BlockSpec((4, TILES, 16, 128), lambda d: (d, 0, 0, 0)), whole, whole, whole],
         out_specs=(whole,) * 4,
-        scratch_shapes=[pltpu.VMEM((FOLD, QROWS, 128), F32), pltpu.VMEM((128, 128), F32)],
+        scratch_shapes=[pltpu.VMEM((FOLD, QROWS, 128), F32), pltpu.VMEM((CPAD, 128), F32), pltpu.VMEM((4, TILES * 16 + 8, 128), F32)],
         compiler_params=pltpu.CompilerParams(vmem_limit_bytes=48 * 2**20),
         name="match",
-    )(wt, refs, ctf, jnp.asarray(fwd), jnp.asarray(bwd))
+    )(group, wt, refs, ctf, jnp.asarray(fwd), jnp.asarray(bwd))
 
 COMBOS = [(ry, c) for ry in (1, 0) for c in (2, 1, 3, 0)]
 BLOCKS = [(2, 1), (2, 0), (1, 1), (3, 1), (1, 0), (3, 0), (0, 1), (0, 0)]
@@ -481,7 +509,7 @@
     def send(t, half, stage, combo, kind):
         axis = axes_of(half)[::-1][stage]
         sign = 1 if kind in ("a0", "l0", "l1", "y") else -1
-        size = 1.0 if kind == "y" else SUB[int(kind[1])] / sum(SUB)
+        size = share(half, None if kind == "y" else int(kind[1]))
         msg = (half, stage, combo, kind)
         steps.append((t, "send", msg))
         links.send(t, axis, sign, size, msg)
@@ -555,6 +583,12 @@
     return steps, {s[2]: i for i, s in enumerate(s for s in steps if s[1] == "send")}
 
 
+def inner(half, sub):
+    low, mid, high = PARTS[half]
+    first, end = ((low, high), (low, mid), (mid, high))[0 if sub is None else sub + 1]
+    return pl.ds(first - low, end - first)
+
+
 class Scatter:
     def __init__(self, me, own, three, pair, out, send_sem, recv_sem):
         self.me, self.own, self.three, self.pair, self.out = me, own, three, pair, out
@@ -565,35 +599,35 @@
     def group(self, stage, combo):
         return 8 if stage == 2 else COMBOS.index(combo)
 
-    def mine(self, half, stage, combo, k):
+    def mine(self, half, stage, combo, k, sub=None):
         if stage == 2:
-            return self.pair.at[half, k]
+            return self.pair.at[half, k, inner(half, sub)]
         order = axes_of(half)[::-1]
         rel = [0, 0, 0]
         rel[order[0]] = k
         rel[1] = combo[0]
         rel[order[2]] = combo[1]
-        return self.own.at[slot(self.me, rel), half]
+        return self.own.at[slot(self.me, rel), span(half, sub)]
 
     def box(self, msg):
         half, stage, combo, kind = msg
         if kind == "y":
-            return self.pair.at[half, combo]
+            return self.pair.at[half, combo, inner(half, None)]
         which = {"a": 0, "l": 1, "r": 2}[kind[0]]
-        return self.three.at[half, self.group(stage, combo), which, span(int(kind[1]))]
+        return self.three.at[half, self.group(stage, combo), which, inner(half, int(kind[1]))]
 
     def source(self, msg):
         half, stage, combo, kind = msg
         if kind == "y":
-            return self.three.at[half, self.group(0, (1, combo)), 1]
-        where = span(int(kind[1]))
+            return self.three.at[half, self.group(0, (1, combo)), 1, inner(half, None)]
+        sub = int(kind[1])
         if kind in ("a0", "a1"):
-            return self.mine(half, stage, combo, 2).at[where]
+            return self.mine(half, stage, combo, 2, sub)
         if kind == "l1":
-            return self.mine(half, stage, combo, 1).at[where]
+            return self.mine(half, stage, combo, 1, sub)
         if kind == "r0":
-            return self.mine(half, stage, combo, 3).at[where]
-        return self.three.at[half, self.group(stage, combo), 0, where]
+            return self.mine(half, stage, combo, 3, sub)
+        return self.three.at[half, self.group(stage, combo), 0, inner(half, sub)]
 
     def copy(self, msg, src=None):
         half, stage, combo, kind = msg
@@ -611,14 +645,10 @@
         )
 
     def add(self, dst, terms, count):
-        def one(i, carry):
-            value = terms[0][i].astype(F32)
-            for term in terms[1:]:
-                value = value + term[i].astype(F32)
-            dst[i] = value.astype(dst.dtype)
-            return carry
-
-        lax.fori_loop(0, count, one, 0)
+        value = terms[0][0:count].astype(F32)
+        for term in terms[1:]:
+            value = value + term[0:count].astype(F32)
+        dst[0:count] = value.astype(dst.dtype)
 
     def step(self, item):
         _, what, key = item
@@ -630,26 +660,27 @@
         elif what == "relay":
             half, stage, combo, kind = key
             box = self.box(key)
-            mine = self.mine(half, stage, combo, 1 if kind == "a0" else 3).at[span(int(kind[1]))]
-            self.add(box, (mine, box), SUB[int(kind[1])])
+            sub = int(kind[1])
+            mine = self.mine(half, stage, combo, 1 if kind == "a0" else 3, sub)
+            self.add(box, (mine, box), inner(half, sub).size)
         elif what == "pair":
             half, c = key
             box = self.pair.at[half, c]
-            self.add(box, (self.three.at[half, self.group(0, (0, c)), 1], box), sum(SUB))
+            self.add(box, (self.three.at[half, self.group(0, (0, c)), 1], box), inner(half, None).size)
         else:
             half, stage, combo = key
             left = self.three.at[half, self.group(stage, combo), 1]
             right = self.three.at[half, self.group(stage, combo), 2]
             mine = self.mine(half, stage, combo, 0)
-            dst = self.out.at[half] if stage == 2 else left
-            self.add(dst, (mine, left, right), sum(SUB))
+            dst = self.out.at[span(half, None)] if stage == 2 else left
+            self.add(dst, (mine, left, right), inner(half, None).size)
 
     def finish(self):
         for key in self.sent:
             self.copy(key, self.source(key)).wait_send()
 
 
-def back_kernel(wt, spec, stat, out, logz, own, three, pair, tab, seen, send_sem, recv_sem, stat_send, stat_recv):
+def back_kernel(classes, wt, spec, stat, out, logz, own, three, pair, tab, flat, seen, send_sem, recv_sem, stat_send, stat_recv):
     i = pl.program_id(0)
     me = place()
     x, y, z, cls = me
@@ -701,12 +732,15 @@
         dz = jnp.where(i == at, bz, dz)
         dy = jnp.where(i == at, by, dy)
     base = (((z + dz) % 4) * 2 + (y + dy) % 2) * 4
-    for r in range(ROTS):
-        g, sg = fold_of(r)
-        both = jnp.dot(tab[g], wt[r], preferred_element_type=F32)
-        a, b = both[:CPAD], both[CPAD:]
-        own[base + r // 9, 0, r % 9] = (a[:, :128] - sg * b[:, 128:]).astype(BF16)
-        own[base + r // 9, 1, r % 9] = (a[:, 128:] + sg * b[:, :128]).astype(BF16)
+    for o in range(4):
+        for j in range(9):
+            g, sg = fold_of(o * 9 + j)
+            both = jnp.dot(tab[g], wt[o * 9 + j], preferred_element_type=F32)
+            a, b = both[:CPAD], both[CPAD:]
+            rows = CPAD if j < 8 else HALF_ROWS - 8 * classes
+            flat[o, 0, pl.ds(j * classes, rows), :] = (a[:, :128] - sg * b[:, 128:])[:rows]
+            flat[o, 1, pl.ds(j * classes, rows), :] = (a[:, 128:] + sg * b[:, :128])[:rows]
+        own[base + o] = flat[o].astype(BF16).reshape(TILES, 16, 128)
 
     for at in range(len(BLOCKS)):
 
@@ -728,22 +762,23 @@
     return ((dp // 8 + dz) % 4) * 2 + ((dp // 4) % 2 + dy) % 2, 0, 0
 
 
-def back(wt, spec, stat):
+def back(wt, spec, stat, classes):
     steps, index = scatter_keys()
     whole = pl.BlockSpec(memory_space=pltpu.VMEM)
     owners = SIZES[0] * SIZES[1] * SIZES[2]
-    block = (ANGLES // owners, CPAD, 128)
+    half = (TILES // 2 + 1, 16, 128)
     return pl.pallas_call(
-        back_kernel,
+        functools.partial(back_kernel, classes),
         grid=(len(BLOCKS),),
-        out_shape=(jax.ShapeDtypeStruct((2,) + block, F32), jax.ShapeDtypeStruct((8, 128), F32)),
+        out_shape=(jax.ShapeDtypeStruct((TILES, 16, 128), F32), jax.ShapeDtypeStruct((8, 128), F32)),
         in_specs=[pl.BlockSpec((ROTS, QROWS, 256), block_index), whole, whole],
         out_specs=(whole, whole),
         scratch_shapes=[
-            pltpu.VMEM((owners, 2) + block, BF16),
-            pltpu.VMEM((2, 9, 3) + block, BF16),
-            pltpu.VMEM((2, 4) + block, BF16),
+            pltpu.VMEM((owners, TILES, 16, 128), BF16),
+            pltpu.VMEM((2, 9, 3) + half, BF16),
+            pltpu.VMEM((2, 4) + half, BF16),
             pltpu.VMEM((FOLD, 128, QROWS), BF16),
+            pltpu.VMEM((4, 2, HALF_ROWS, 128), F32),
             pltpu.VMEM((3, 2, 8, 128), F32),
             pltpu.SemaphoreType.DMA((len(index),)),
             pltpu.SemaphoreType.DMA((len(index),)),
@@ -766,37 +801,33 @@
 def twist_refs(references, cos, sin):
     re = references[:, 0].astype(F32)
     im = references[:, 1].astype(F32)
-    both = jnp.stack([re * cos + im * sin, im * cos - re * sin], 1)
-    both = jnp.pad(both, ((0, 0), (0, 0), (0, CPAD - both.shape[2]), (0, 0))).astype(BF16)
-    both = both.reshape(both.shape[0], 2 * CPAD, 2, 64)
-    return jnp.transpose(both, (2, 0, 3, 1))
-
-
-def untwist(sums, cos, sin, classes):
-    re = sums[0, :, :classes].astype(F32)
-    im = sums[1, :, :classes].astype(F32)
+    both = jnp.stack([re * cos + im * sin, im * cos - re * sin], 0).astype(BF16)
+    both = both.reshape(2, -1, both.shape[3])
+    both = jnp.pad(both, ((0, 0), (0, HALF_ROWS - both.shape[1]), (0, 0)))
+    return both.reshape(TILES, 16, both.shape[2])
+
+
+def untwist(sums, cos, sin, block, classes):
+    rows = sums.reshape(2, HALF_ROWS, -1)[:, : block * classes].reshape(2, block, classes, -1)
+    re, im = rows[0], rows[1]
     return jnp.stack([re * cos - im * sin, re * sin + im * cos], 1)
 
 
 def order_angles(particles):
     return jnp.concatenate([particles[:, :, 0::2], particles[:, :, 1::2]], 2)
-
-
-def group_rows(defocus_group, ctf_table):
-    hit = defocus_group[:, None] == jnp.arange(ctf_table.shape[0], dtype=jnp.int32)[None, :]
-    return jnp.sum(jnp.where(hit[:, :, None], ctf_table[None], 0.0), 1)
 
 
 def local(particles, references, ctf_table, rot_offset, prior_shift, defocus_group):
     block, _, classes = references.shape[:3]
     freq = lax.axis_index("dp") * block + jnp.arange(block, dtype=jnp.int32)
     cos, sin = twist_tables(freq, rot_offset)
-    ctf = group_rows(defocus_group, ctf_table)
-    wt, refs = transform(prior_shift, order_angles(particles), ctf, twist_refs(references, cos, sin))
-    spec, peak, mass, post = match(wt, refs, ctf, classes)
-    sums, total = back(wt, spec, jnp.stack([peak, mass]))
+    wt, refs = transform(
+        prior_shift, defocus_group, order_angles(particles), ctf_table, twist_refs(references, cos, sin)
+    )
+    spec, peak, mass, post = match(defocus_group, wt, refs, ctf_table, classes)
+    sums, total = back(wt, spec, jnp.stack([peak, mass]), classes)
     posterior = post[:, :classes] * jnp.exp(peak[:, :classes] - total[:, :classes])
-    return total[:, 0], posterior, untwist(sums, cos, sin, classes)
+    return total[:, 0], posterior, untwist(sums, cos, sin, block, classes)
 
 
 def solution(mesh):

time: 162 us -> 146 us (0.901)
  Pallas kernels: 149 us -> 134 us
  local copies, waits for them, and re-layouts: 7.06 us -> 4.42 us
    pallas_call x1, Pallas kernels: 61.6 us -> 52.1 us  [back(): pl.pallas_call(functools.partial(back_kernel, classes), grid=(len(BLOCKS)...]
    pallas_call x1, Pallas kernels: 24.5 us -> 21.2 us  [match(): pl.pallas_call(functools.partial(match_kernel, classes), grid=(ANGLES //...]
    pallas_call x1, Pallas kernels: 63 us -> 60.7 us  [transform(): pl.pallas_call(transform_kernel, grid=(STEPS,), out_shape=(jax.ShapeDtype...]
where the time goes in v3:
time: 146 us
  Pallas kernels  134 us (92%)
  other arithmetic  6.43 us (4%)
  local copies, waits for them, and re-layouts  4.42 us (3%)
    pallas_call x1, Pallas kernels, transform(): pl.pallas_call(transform_kernel, grid=(STEPS,), out_shape=(jax.ShapeDtype...  60.7 us
    pallas_call x1, Pallas kernels, back(): pl.pallas_call(functools.partial(back_kernel, classes), grid=(len(BLOCKS)...  52.1 us
    pallas_call x1, Pallas kernels, match(): pl.pallas_call(functools.partial(match_kernel, classes), grid=(ANGLES //...  21.2 us

profile of v3, /device:TPU:0, one launch (start us, length us, event | category | flops | bytes accessed | tf_op | source)
XLA Modules:
  0.0 145.6 jit_solution(3430958923201108417)
XLA Ops:
  0.6 0.0 copy-start.4
  0.6 1.6 %fusion.15 = (bf16[9,1,50,128]{3,1,2,0:T(2,128)(2,1)S(1)}, bf16[9,1,50,128]{3,1,2,0:T(2,128)(2,1)S(1)}) fusion(bf16[9,2,50,128]{3,1,2,0:T(2,128)(2,1)} %param.13), kind=kLoop, calls=%fused_computation.31 | loop fusion | bytes 460800 | tf_op jit(solution)/shard_map/slice | solution.py:802
  2.2 0.5 bitcast_convert_fusion
  2.7 0.7 multiply_remainder_fusion
  3.5 0.1 rem.24
  3.6 0.2 add_convert_fusion
  3.8 0.7 fusion.2
  4.5 0.0 copy-done.4
  4.5 0.0 copy-start.6
  4.5 0.5 slice.35
  5.0 0.5 slice.36
  5.5 1.1 pad_maximum_fusion.part
  6.6 0.0 copy-done.6
  6.6 0.7 copy.24.shift
  7.3 0.0 copy-start
  7.3 0.0 copy-start.1
  7.3 0.0 copy-start.2
  7.3 0.0 copy-start.3
  7.3 60.7 %transform.1 = (bf16[288,208,256]{2,1,0:T(8,128)(2,1)}, bf16[32,57,16,128]{3,2,1,0:T(8,128)(2,1)}) custom-call(s32[8,2]{1,0:T(8,128)} %copy.24.shift, s32[8]{0:T(128)} %group.3, bf16[8,2,288,128]{3,2,1,0:T(8,128)(2,1)} %pad_maximum_fusion.part, f32[16,128]{1,0:T(8,128)} %ctf.3, f32[11,2,288,128]{3,2,1,0:T(8,128)} %constant.37.clone.txh, ...), custom_call_target="tpu_custom_call" | custom-call | tf_op jit(solution)/shard_map/transform/pallas_call | solution.py:346
  68.0 0.0 copy-done
  68.0 0.0 copy-done.1
  68.0 0.0 copy-done.2
  68.0 0.0 copy-done.3
  68.0 21.2 %match.1 = (f32[19,208,128]{2,1,0:T(8,128)S(1)}, f32[8,128]{1,0:T(8,128)S(1)}, f32[8,128]{1,0:T(8,128)S(1)}, f32[8,128]{1,0:T(8,128)S(1)}) custom-call(s32[8]{0:T(128)S(1)} %copy-done.3, bf16[288,208,256]{2,1,0:T(8,128)(2,1)} %get-tuple-element.11.wt, bf16[32,57,16,128]{3,2,1,0:T(8,128)(2,1)} %get-tuple-element.12.refs, f32[16,128]{1,0:T(8,128)S(1)} %copy-done.2, ...), custom_call_target="tpu_custom_call" | custom-call | tf_op jit(solution)/shard_map/match/pallas_call | solution.py:489
  89.2 0.0 copy-start.5
  89.2 52.1 %back.1 = (f32[57,16,128]{2,1,0:T(8,128)S(1)}, f32[8,128]{1,0:T(8,128)S(1)}) custom-call(bf16[288,208,256]{2,1,0:T(8,128)(2,1)} %get-tuple-element.11.wt, f32[19,208,128]{2,1,0:T(8,128)S(1)} %get-tuple-element.13.spec, f32[2,8,128]{2,1,0:T(8,128)S(1)} %pad_maximum_fusion.2.stat), custom_call_target="tpu_custom_call" | custom-call | tf_op jit(solution)/shard_map/back/pallas_call | solution.py:770
  141.3 0.2 copy.27
  141.6 0.2 copy.28
  141.8 0.0 copy-done.5
  141.8 0.1 fusion.8
  142.0 1.2 multiply_subtract_fusion
  143.2 1.2 pad_maximum_fusion.1
  144.4 0.6 exponential_multiply_fusion
  145.0 0.6 slice_reduce_fusion
  (4 shorter events, 0.1 us)
Async XLA Ops:
  0.6 3.9 %copy-start.4 = (bf16[8,2,288,128]{3,2,1,0:T(8,128)(2,1)S(1)}, bf16[8,2,288,128]{3,2,1,0:T(8,128)(2,1)}, u32[]{:S(2)}) copy-start(bf16[8,2,288,128]{3,2,1,0:T(8,128)(2,1)} %param.12) | copy-start | bytes 3538948
  4.5 2.1 %copy-start.6 = (s32[8,2]{0,1:T(2,128)S(1)}, s32[8,2]{0,1:T(2,128)}, u32[]{:S(2)}) copy-start(s32[8,2]{0,1:T(2,128)} %param.16) | copy-start | bytes 196
  7.3 60.7 %copy-start = (f32[19,19,128]{2,1,0:T(8,128)S(1)}, f32[19,19,128]{2,1,0:T(8,128)}, u32[]{:S(2)}) copy-start(f32[19,19,128]{2,1,0:T(8,128)} %constant.41.clone.fwd) | copy-start | bytes 554500
  7.3 60.7 %copy-start.1 = (f32[19,19,128]{2,1,0:T(8,128)S(1)}, f32[19,19,128]{2,1,0:T(8,128)}, u32[]{:S(2)}) copy-start(f32[19,19,128]{2,1,0:T(8,128)} %constant.42.clone.bwd) | copy-start | bytes 554500
  7.3 60.7 %copy-start.2 = (f32[16,128]{1,0:T(8,128)S(1)}, f32[16,128]{1,0:T(8,128)}, u32[]{:S(2)}) copy-start(f32[16,128]{1,0:T(8,128)} %ctf.3) | copy-start | bytes 24580
  7.3 60.7 %copy-start.3 = (s32[8]{0:T(128)S(1)}, s32[8]{0:T(128)}, u32[]{:S(2)}) copy-start(s32[8]{0:T(128)} %group.3) | copy-start | bytes 100
  89.2 52.6 %copy-start.5 = (s32[50]{0:T(128)S(1)}, s32[50]{0:T(128)}, u32[]{:S(2)}) copy-start(s32[50]{0:T(128)} %param.15) | copy-start | bytes 604

commit v4 on v3

--- a/solution.py
+++ b/solution.py
@@ -18,7 +18,7 @@
 HALF = ANGLES // 2
 REACH = 10
 FOLD = ROTS // 2 + 1
-IPAD = 80
+IPAD = 72
 QROWS = 208
 CPAD = 64
 F32 = jnp.float32
@@ -44,7 +44,10 @@
     for start in (0, 1):
         t = np.arange(start, ANGLES, 2)
         ang = 2.0 * np.pi * ((row[:, None] * t[None, :]) % ANGLES) / ANGLES
-        out.append(np.concatenate([np.cos(ang), np.sin(ang)], 0).astype(np.float32))
+        cos, sin = np.cos(ang), np.sin(ang)
+        quarter = 2.0 * np.pi * ((IPAD * t) % ANGLES) / ANGLES
+        sin[0] = np.rint(np.sin(quarter) if start else np.cos(quarter))
+        out.append(np.concatenate([cos, sin], 0).astype(np.float32))
     return out
 
 
@@ -212,8 +215,8 @@
 
 GROUP = 8
 STEPS = 26
-PITCH = 4 * IPAD + 1
-UNIT_STEPS = 2.06
+PITCH = 4 * IPAD + 3
+UNIT_STEPS = 1.6
 
 
 def transform_kernel(shift, group, part, ctf, txh, tyh, te, to, own, out, store, tx, ty, z1, xs, fr, fi, send_sem, recv_sem, own_sem, tab_sem):
@@ -292,14 +295,25 @@
             lo, hi = slice(256 * p, 256 * p + 128), slice(256 * p + 128, 256 * p + 256)
             for c in range(0, IPAD, 8):
                 cos, sin = slice(c, c + 8), slice(IPAD + c, IPAD + c + 8)
-                u1 = (even[cos, lo] + even[sin, hi]) * gain
-                u2 = (even[cos, lo] - even[sin, hi]) * gain
-                w1 = (even[cos, hi] - even[sin, lo]) * gain
-                w2 = (even[cos, hi] + even[sin, lo]) * gain
-                v1 = (odd[cos, lo] + odd[sin, hi]) * gain
-                v2 = (odd[cos, lo] - odd[sin, hi]) * gain
-                y1 = (odd[cos, hi] - odd[sin, lo]) * gain
-                y2 = (odd[cos, hi] + odd[sin, lo]) * gain
+                er, ei, fr_, fi_ = even[cos, lo], even[cos, hi], even[sin, lo], even[sin, hi]
+                gr, gi, hr, hi_ = odd[cos, lo], odd[cos, hi], odd[sin, lo], odd[sin, hi]
+                if c == 0:
+                    for at, re, im in (
+                        (0, fr_[0:1] + hi_[0:1], fi_[0:1] - hr[0:1]),
+                        (1, fr_[0:1] - hi_[0:1], fi_[0:1] + hr[0:1]),
+                    ):
+                        fr[pl.ds(j * PITCH + 4 * IPAD + at, 1), :] = re * gain
+                        fi[pl.ds(j * PITCH + 4 * IPAD + at, 1), :] = im * gain
+                    rest = lax.broadcasted_iota(jnp.int32, (8, 128), 0) > 0
+                    fr_, fi_, hr, hi_ = [jnp.where(rest, v, 0.0) for v in (fr_, fi_, hr, hi_)]
+                u1 = (er + fi_) * gain
+                u2 = (er - fi_) * gain
+                w1 = (ei - fr_) * gain
+                w2 = (ei + fr_) * gain
+                v1 = (gr + hi_) * gain
+                v2 = (gr - hi_) * gain
+                y1 = (gi - hr) * gain
+                y2 = (gi + hr) * gain
                 for blk, (re, im) in enumerate(
                     ((u1 + v1, w1 + y1), (u1 - v1, w1 - y1), (u2 - v2, w2 - y2), (u2 + v2, w2 + y2))
                 ):
@@ -323,8 +337,8 @@
 
         emit(0, 0, 0)
         emit(0, 1, HALF)
-        emit(HALF // 2, 0, HALF // 2)
-        emit(HALF // 2, 1, HALF + HALF // 2)
+        emit(0, 4, IPAD)
+        emit(1, 4, HALF + IPAD)
         lax.fori_loop(1, HALF // 2, pack, 0, unroll=8)
 
     @pl.when(u == STEPS - 1)
@@ -500,7 +514,7 @@
 
 COMBOS = [(ry, c) for ry in (1, 0) for c in (2, 1, 3, 0)]
 BLOCKS = [(2, 1), (2, 0), (1, 1), (3, 1), (1, 0), (3, 0), (0, 1), (0, 0)]
-BLOCK_UNITS = 0.6
+BLOCK_UNITS = 0.9
 
 
 def scatter_plan():

time: 146 us -> 145 us (level)
  no operation moved by 1% of the time
where the time goes in v4:
time: 145 us; the launch traced here: 144 us
  Pallas kernels  133 us (92%)
  other arithmetic  6.43 us (4%)
  local copies, waits for them, and re-layouts  4.42 us (3%)
    pallas_call x1, Pallas kernels, transform(): pl.pallas_call(transform_kernel, grid=(STEPS,), out_shape=(jax.ShapeDtype...  59.4 us
    pallas_call x1, Pallas kernels, back(): pl.pallas_call(functools.partial(back_kernel, classes), grid=(len(BLOCKS)...  52.2 us
    pallas_call x1, Pallas kernels, match(): pl.pallas_call(functools.partial(match_kernel, classes), grid=(ANGLES //...  21.2 us

profile of v4, /device:TPU:0, one launch (start us, length us, event | category | flops | bytes accessed | tf_op | source)
XLA Modules:
  0.0 144.4 jit_solution(15091698412372108199)
XLA Ops:
  0.6 0.0 copy-start.4
  0.6 1.6 %fusion.15 = (bf16[9,1,50,128]{3,1,2,0:T(2,128)(2,1)S(1)}, bf16[9,1,50,128]{3,1,2,0:T(2,128)(2,1)S(1)}) fusion(bf16[9,2,50,128]{3,1,2,0:T(2,128)(2,1)} %param.13), kind=kLoop, calls=%fused_computation.31 | loop fusion | bytes 460800 | tf_op jit(solution)/shard_map/slice | solution.py:816
  2.2 0.5 bitcast_convert_fusion
  2.7 0.7 multiply_remainder_fusion
  3.5 0.1 rem.24
  3.6 0.2 add_convert_fusion
  3.8 0.7 fusion.2
  4.5 0.0 copy-done.4
  4.5 0.0 copy-start.6
  4.5 0.5 slice.35
  5.0 0.5 slice.36
  5.5 1.1 pad_maximum_fusion.part
  6.6 0.0 copy-done.6
  6.6 0.7 copy.24.shift
  7.3 0.0 copy-start
  7.3 0.0 copy-start.1
  7.3 0.0 copy-start.2
  7.3 0.0 copy-start.3
  7.3 59.4 %transform.1 = (bf16[288,208,256]{2,1,0:T(8,128)(2,1)}, bf16[32,57,16,128]{3,2,1,0:T(8,128)(2,1)}) custom-call(s32[8,2]{1,0:T(8,128)} %copy.24.shift, s32[8]{0:T(128)} %group.3, bf16[8,2,288,128]{3,2,1,0:T(8,128)(2,1)} %pad_maximum_fusion.part, f32[16,128]{1,0:T(8,128)} %ctf.3, f32[11,2,288,128]{3,2,1,0:T(8,128)} %constant.37.clone.txh, ...), custom_call_target="tpu_custom_call" | custom-call | tf_op jit(solution)/shard_map/transform/pallas_call | solution.py:360
  66.7 0.0 copy-done
  66.7 0.0 copy-done.1
  66.7 0.0 copy-done.2
  66.7 0.0 copy-done.3
  66.7 21.2 %match.1 = (f32[19,208,128]{2,1,0:T(8,128)S(1)}, f32[8,128]{1,0:T(8,128)S(1)}, f32[8,128]{1,0:T(8,128)S(1)}, f32[8,128]{1,0:T(8,128)S(1)}) custom-call(s32[8]{0:T(128)S(1)} %copy-done.3, bf16[288,208,256]{2,1,0:T(8,128)(2,1)} %get-tuple-element.11.wt, bf16[32,57,16,128]{3,2,1,0:T(8,128)(2,1)} %get-tuple-element.12.refs, f32[16,128]{1,0:T(8,128)S(1)} %copy-done.2, ...), custom_call_target="tpu_custom_call" | custom-call | tf_op jit(solution)/shard_map/match/pallas_call | solution.py:503
  87.9 0.0 copy-start.5
  87.9 52.2 %back.1 = (f32[57,16,128]{2,1,0:T(8,128)S(1)}, f32[8,128]{1,0:T(8,128)S(1)}) custom-call(bf16[288,208,256]{2,1,0:T(8,128)(2,1)} %get-tuple-element.11.wt, f32[19,208,128]{2,1,0:T(8,128)S(1)} %get-tuple-element.13.spec, f32[2,8,128]{2,1,0:T(8,128)S(1)} %pad_maximum_fusion.2.stat), custom_call_target="tpu_custom_call" | custom-call | tf_op jit(solution)/shard_map/back/pallas_call | solution.py:784
  140.2 0.2 copy.27
  140.4 0.2 copy.28
  140.7 0.0 copy-done.5
  140.7 0.1 fusion.8
  140.8 1.2 multiply_subtract_fusion
  142.0 1.2 pad_maximum_fusion.1
  143.2 0.6 exponential_multiply_fusion
  143.8 0.6 slice_reduce_fusion
  (4 shorter events, 0.1 us)
Async XLA Ops:
  0.6 3.9 %copy-start.4 = (bf16[8,2,288,128]{3,2,1,0:T(8,128)(2,1)S(1)}, bf16[8,2,288,128]{3,2,1,0:T(8,128)(2,1)}, u32[]{:S(2)}) copy-start(bf16[8,2,288,128]{3,2,1,0:T(8,128)(2,1)} %param.12) | copy-start | bytes 3538948
  4.5 2.1 %copy-start.6 = (s32[8,2]{0,1:T(2,128)S(1)}, s32[8,2]{0,1:T(2,128)}, u32[]{:S(2)}) copy-start(s32[8,2]{0,1:T(2,128)} %param.16) | copy-start | bytes 196
  7.3 59.4 %copy-start = (f32[19,19,128]{2,1,0:T(8,128)S(1)}, f32[19,19,128]{2,1,0:T(8,128)}, u32[]{:S(2)}) copy-start(f32[19,19,128]{2,1,0:T(8,128)} %constant.41.clone.fwd) | copy-start | bytes 554500
  7.3 59.4 %copy-start.1 = (f32[19,19,128]{2,1,0:T(8,128)S(1)}, f32[19,19,128]{2,1,0:T(8,128)}, u32[]{:S(2)}) copy-start(f32[19,19,128]{2,1,0:T(8,128)} %constant.42.clone.bwd) | copy-start | bytes 554500
  7.3 59.4 %copy-start.2 = (f32[16,128]{1,0:T(8,128)S(1)}, f32[16,128]{1,0:T(8,128)}, u32[]{:S(2)}) copy-start(f32[16,128]{1,0:T(8,128)} %ctf.3) | copy-start | bytes 24580
  7.3 59.4 %copy-start.3 = (s32[8]{0:T(128)S(1)}, s32[8]{0:T(128)}, u32[]{:S(2)}) copy-start(s32[8]{0:T(128)} %group.3) | copy-start | bytes 100
  87.9 52.8 %copy-start.5 = (s32[50]{0:T(128)S(1)}, s32[50]{0:T(128)}, u32[]{:S(2)}) copy-start(s32[50]{0:T(128)} %param.15) | copy-start | bytes 604

commit v5 on v4

--- a/solution.py
+++ b/solution.py
@@ -514,7 +514,7 @@
 
 COMBOS = [(ry, c) for ry in (1, 0) for c in (2, 1, 3, 0)]
 BLOCKS = [(2, 1), (2, 0), (1, 1), (3, 1), (1, 0), (3, 0), (0, 1), (0, 0)]
-BLOCK_UNITS = 0.9
+BLOCK_UNITS = 1.2
 
 
 def scatter_plan():

time: 145 us -> 144 us (level)
  no operation moved by 1% of the time
where the time goes in v5:
time: 144 us
  Pallas kernels  132 us (92%)
  other arithmetic  6.43 us (4%)
  local copies, waits for them, and re-layouts  4.42 us (3%)
    pallas_call x1, Pallas kernels, transform(): pl.pallas_call(transform_kernel, grid=(STEPS,), out_shape=(jax.ShapeDtype...  59.4 us
    pallas_call x1, Pallas kernels, back(): pl.pallas_call(functools.partial(back_kernel, classes), grid=(len(BLOCKS)...  51.7 us
    pallas_call x1, Pallas kernels, match(): pl.pallas_call(functools.partial(match_kernel, classes), grid=(ANGLES //...  21.2 us

profile of v5, /device:TPU:0, one launch (start us, length us, event | category | flops | bytes accessed | tf_op | source)
XLA Modules:
  0.0 143.9 jit_solution(16482132214311070638)
XLA Ops:
  0.6 0.0 copy-start.4
  0.6 1.6 %fusion.15 = (bf16[9,1,50,128]{3,1,2,0:T(2,128)(2,1)S(1)}, bf16[9,1,50,128]{3,1,2,0:T(2,128)(2,1)S(1)}) fusion(bf16[9,2,50,128]{3,1,2,0:T(2,128)(2,1)} %param.13), kind=kLoop, calls=%fused_computation.31 | loop fusion | bytes 460800 | tf_op jit(solution)/shard_map/slice | solution.py:816
  2.2 0.5 bitcast_convert_fusion
  2.7 0.7 multiply_remainder_fusion
  3.5 0.1 rem.24
  3.6 0.2 add_convert_fusion
  3.8 0.7 fusion.2
  4.5 0.0 copy-done.4
  4.5 0.0 copy-start.6
  4.5 0.5 slice.35
  5.0 0.5 slice.36
  5.5 1.1 pad_maximum_fusion.part
  6.6 0.0 copy-done.6
  6.6 0.7 copy.24.shift
  7.3 0.0 copy-start
  7.3 0.0 copy-start.1
  7.3 0.0 copy-start.2
  7.3 0.0 copy-start.3
  7.3 59.4 %transform.1 = (bf16[288,208,256]{2,1,0:T(8,128)(2,1)}, bf16[32,57,16,128]{3,2,1,0:T(8,128)(2,1)}) custom-call(s32[8,2]{1,0:T(8,128)} %copy.24.shift, s32[8]{0:T(128)} %group.3, bf16[8,2,288,128]{3,2,1,0:T(8,128)(2,1)} %pad_maximum_fusion.part, f32[16,128]{1,0:T(8,128)} %ctf.3, f32[11,2,288,128]{3,2,1,0:T(8,128)} %constant.37.clone.txh, ...), custom_call_target="tpu_custom_call" | custom-call | tf_op jit(solution)/shard_map/transform/pallas_call | solution.py:360
  66.7 0.0 copy-done
  66.7 0.0 copy-done.1
  66.7 0.0 copy-done.2
  66.7 0.0 copy-done.3
  66.7 21.2 %match.1 = (f32[19,208,128]{2,1,0:T(8,128)S(1)}, f32[8,128]{1,0:T(8,128)S(1)}, f32[8,128]{1,0:T(8,128)S(1)}, f32[8,128]{1,0:T(8,128)S(1)}) custom-call(s32[8]{0:T(128)S(1)} %copy-done.3, bf16[288,208,256]{2,1,0:T(8,128)(2,1)} %get-tuple-element.11.wt, bf16[32,57,16,128]{3,2,1,0:T(8,128)(2,1)} %get-tuple-element.12.refs, f32[16,128]{1,0:T(8,128)S(1)} %copy-done.2, ...), custom_call_target="tpu_custom_call" | custom-call | tf_op jit(solution)/shard_map/match/pallas_call | solution.py:503
  87.9 0.0 copy-start.5
  87.9 51.7 %back.1 = (f32[57,16,128]{2,1,0:T(8,128)S(1)}, f32[8,128]{1,0:T(8,128)S(1)}) custom-call(bf16[288,208,256]{2,1,0:T(8,128)(2,1)} %get-tuple-element.11.wt, f32[19,208,128]{2,1,0:T(8,128)S(1)} %get-tuple-element.13.spec, f32[2,8,128]{2,1,0:T(8,128)S(1)} %pad_maximum_fusion.2.stat), custom_call_target="tpu_custom_call" | custom-call | tf_op jit(solution)/shard_map/back/pallas_call | solution.py:784
  139.6 0.2 copy.27
  139.9 0.2 copy.28
  140.1 0.0 copy-done.5
  140.1 0.1 fusion.8
  140.3 1.2 multiply_subtract_fusion
  141.5 1.2 pad_maximum_fusion.1
  142.7 0.6 exponential_multiply_fusion
  143.3 0.6 slice_reduce_fusion
  (4 shorter events, 0.1 us)
Async XLA Ops:
  0.6 3.9 %copy-start.4 = (bf16[8,2,288,128]{3,2,1,0:T(8,128)(2,1)S(1)}, bf16[8,2,288,128]{3,2,1,0:T(8,128)(2,1)}, u32[]{:S(2)}) copy-start(bf16[8,2,288,128]{3,2,1,0:T(8,128)(2,1)} %param.12) | copy-start | bytes 3538948
  4.5 2.1 %copy-start.6 = (s32[8,2]{0,1:T(2,128)S(1)}, s32[8,2]{0,1:T(2,128)}, u32[]{:S(2)}) copy-start(s32[8,2]{0,1:T(2,128)} %param.16) | copy-start | bytes 196
  7.3 59.4 %copy-start = (f32[19,19,128]{2,1,0:T(8,128)S(1)}, f32[19,19,128]{2,1,0:T(8,128)}, u32[]{:S(2)}) copy-start(f32[19,19,128]{2,1,0:T(8,128)} %constant.41.clone.fwd) | copy-start | bytes 554500
  7.3 59.4 %copy-start.1 = (f32[19,19,128]{2,1,0:T(8,128)S(1)}, f32[19,19,128]{2,1,0:T(8,128)}, u32[]{:S(2)}) copy-start(f32[19,19,128]{2,1,0:T(8,128)} %constant.42.clone.bwd) | copy-start | bytes 554500
  7.3 59.4 %copy-start.2 = (f32[16,128]{1,0:T(8,128)S(1)}, f32[16,128]{1,0:T(8,128)}, u32[]{:S(2)}) copy-start(f32[16,128]{1,0:T(8,128)} %ctf.3) | copy-start | bytes 24580
  7.3 59.4 %copy-start.3 = (s32[8]{0:T(128)S(1)}, s32[8]{0:T(128)}, u32[]{:S(2)}) copy-start(s32[8]{0:T(128)} %group.3) | copy-start | bytes 100
  87.9 52.2 %copy-start.5 = (s32[50]{0:T(128)S(1)}, s32[50]{0:T(128)}, u32[]{:S(2)}) copy-start(s32[50]{0:T(128)} %param.15) | copy-start | bytes 604
